TPU v7x, 512 devices: a whole 4x8x8 slice. The times are simulated.
512 devices in a mesh: user: 64 (over z, y), item: 8 (over x, core).
Axes of the slice: x: 4, y: 8, z: 8, core: 2. Of those that a mesh axis runs over, the one named last changes fastest.
Arguments:
- tile_values: bfloat16 [7168, 1024, 128], P('user', 'item')
- tile_coords: int32 [7168, 16], P('user', 'item'), may hold values from 0 to 31, as said below
- tile_counts: int32 [64, 8], P('user', 'item'), may hold values from 28 to 112, as said below
- omega: bfloat16 [32768, 128], P('item')
Outputs:
- scaled_q: float32 [262144, 128], P(('user', 'item'))
- scaled_r: float32 [128, 128], replicated
- first_r: float32 [128, 128], replicated
Inputs may be any that keep to these rules, and one draw needn't show every extreme that they name: `tile_coords`: within one device block the slots name distinct tiles; the first of a pair is below 32, the second below 32; slots at or past the block's count are not part of A. `tile_counts`: some device block uses all 112 slots.
All inputs are finite; a program needn't handle non-finite values.
Results may differ from a plain program's by a relative error of at most 0.00035.
Values may be sent and summed in bfloat16 or wider, within the bound.
No kernel may reach another device: no remote copies, remote signals or barrier semaphores. Data moves between devices by JAX's collectives and lax.ppermute only.
A program may use at most 64 MiB of HBM per device.

v0:
```python
import jax
import jax.numpy as jnp
from jax import lax
from jax.sharding import PartitionSpec as P

RB = 32


def right_solve(lower, rows):
    return lax.linalg.triangular_solve(lower, rows, left_side=False, lower=True, transpose_a=True)


def accumulate(total, tiles, places, blocks, start_slot, stop_slot, offset):
    group = 8
    first = start_slot // group
    last = (stop_slot + group - 1) // group
    targets = jnp.arange(total.shape[0], dtype=jnp.int32)

    def turn(step, total):
        begin = step * group
        piece = lax.dynamic_slice_in_dim(tiles, begin, group, 0)
        placed = lax.dynamic_slice_in_dim(places, begin, group, 0)
        chosen = blocks[placed[:, 1]]
        product = jnp.einsum("sij,sjk->sik", piece, chosen, preferred_element_type=jnp.float32)
        slot_ids = begin + jnp.arange(group, dtype=jnp.int32)
        live = ((slot_ids >= start_slot) & (slot_ids < stop_slot)).astype(jnp.float32)
        onehot = (placed[:, 0][:, None] + offset == targets[None, :]).astype(jnp.float32) * live[
            :, None
        ]
        return total + jnp.einsum("sr,sik->rik", onehot, product, precision=lax.Precision.HIGHEST)

    return lax.fori_loop(first, last, turn, total)


def gram_of(rows):
    return jnp.einsum("rk,rl->kl", rows, rows, precision=lax.Precision.HIGHEST)


def per_device(tile_values, tile_coords, tile_counts, omega):
    tile = tile_values.shape[2]
    width = omega.shape[1]
    blocks = omega.reshape(omega.shape[0] // tile, tile, width)
    count = tile_counts[0, 0]
    empty = jnp.zeros((RB, tile, width), jnp.float32)
    summed = accumulate(empty, tile_values, tile_coords, blocks, 0, count, 0)
    partial_rows = summed.reshape(RB * tile, width)
    total_rows = RB * tile * lax.axis_size("user")
    scale = jnp.sqrt(jnp.float32(total_rows))
    sketch = lax.psum(partial_rows, "item")
    lower_one = jnp.linalg.cholesky(lax.psum(gram_of(sketch), "user"))
    basis_one = right_solve(lower_one, sketch)
    lower_two = jnp.linalg.cholesky(lax.psum(gram_of(basis_one), "user"))
    whole_basis = right_solve(lower_two, basis_one)
    share = whole_basis.shape[0] // lax.axis_size("item")
    basis = lax.dynamic_slice_in_dim(whole_basis, lax.axis_index("item") * share, share, 0)
    factor = jnp.dot(lower_two.T, lower_one.T, precision=lax.Precision.HIGHEST)
    return (basis * scale, factor / scale, lower_one.T / scale)


def solution(mesh):
    return jax.shard_map(
        per_device,
        mesh=mesh,
        in_specs=(P("user", "item", None), P("user", "item"), P("user", "item"), P("item", None)),
        out_specs=(P(("user", "item"), None), P(), P()),
        check_vma=False,
    )
```

profile of v0, /device:TPU:1, one launch (start us, length us, event | category | flops | bytes accessed | tf_op | source)
XLA Modules:
  0.0 541.9 jit_solution(12032561962741868594)
XLA Ops:
  8.2 68.9 %while.11 = (s32[]{:T(128)}, f32[32,128,128]{2,0,1:T(8,128)S(1)}, s32[]{:T(128)}, s32[112,2]{0,1:T(2,128)S(1)}, s32[]{:T(128)}, /*index=5*/bf16[112,128,128]{2,1...) while((s32[]{:T(128)}, f32[32,128,128]{2,0,1:T(8,128)S(1)}, ...), condition=%wide.region_1.2_spmd.clone, body=%wide.region_0.1_spmd.clone.sunk | while | flops 84411968 | bytes 6296139 | solution.py:32
  8.3 1.8 gather_fusion
  10.1 1.2 fusion.49
  11.3 0.7 and_convert_fusion.2
  11.9 2.5 convolution_add_fusion.2
  14.5 1.8 gather_fusion
  16.4 1.2 fusion.49
  17.5 0.7 and_convert_fusion.2
  18.2 2.5 convolution_add_fusion.2
  20.8 1.8 gather_fusion
  22.6 1.2 fusion.49
  23.8 0.7 and_convert_fusion.2
  24.5 2.5 convolution_add_fusion.2
  27.1 1.8 gather_fusion
  28.9 1.2 fusion.49
  30.1 0.7 and_convert_fusion.2
  30.7 2.5 convolution_add_fusion.2
  33.3 1.8 gather_fusion
  35.1 1.2 fusion.49
  36.3 0.7 and_convert_fusion.2
  37.0 2.5 convolution_add_fusion.2
  39.6 1.8 gather_fusion
  41.4 1.2 fusion.49
  42.6 0.7 and_convert_fusion.2
  43.2 2.5 convolution_add_fusion.2
  45.8 1.8 gather_fusion
  47.7 1.2 fusion.49
  48.8 0.7 and_convert_fusion.2
  49.5 2.5 convolution_add_fusion.2
  52.1 1.8 gather_fusion
  53.9 1.2 fusion.49
  55.1 0.7 and_convert_fusion.2
  55.8 2.5 convolution_add_fusion.2
  58.3 1.8 gather_fusion
  60.2 1.2 fusion.49
  62.0 2.5 convolution_add_fusion.2
  64.6 1.8 gather_fusion
  66.4 1.2 fusion.49
  68.3 2.5 convolution_add_fusion.2
  70.9 1.8 gather_fusion
  72.7 1.2 fusion.49
  74.5 2.5 convolution_add_fusion.2
  77.0 2.5 copy.13
  79.6 98.7 %all-reduce.4.cloned.1.call-done = f32[4096,128]{1,0:T(8,128)} async-done(((f32[4096,128]{1,0:T(8,128)}), f32[4096,128]{1,0:T(8,128)}) %all-reduce.4.cloned.1.call-update) | async-done | bytes 2097168 | tf_op jit(solution)/shard_map/psum | solution.py:49
  178.3 6.3 %fusion.31 = f32[128,128]{0,1:T(8,128)} fusion(f32[4096,128]{1,0:T(8,128)} %all-reduce.4.cloned.1.call-done), kind=kOutput, calls=%fused_computation.49 | convolution fusion | flops 805306368 | bytes 2162688 | tf_op jit(solution)/shard_map/rk,rl->kl/dot_general | solution.py:36
  184.9 145.6 %all-reduce.6.cloned.1.call-done = f32[128,128]{0,1:T(8,128)} async-done(((f32[128,128]{0,1:T(8,128)}), f32[128,128]{0,1:T(8,128)}) %all-reduce.6.cloned.1.call-update) | async-done | bytes 65552 | tf_op jit(solution)/shard_map/psum | solution.py:50
  330.5 0.9 copy.15
  331.4 0.9 fusion.16
  332.3 11.7 %cholesky.44 = f32[128,128]{1,0:T(8,128)S(1)} custom-call(f32[128,128]{1,0:T(8,128)S(1)} %fusion.16), custom_call_target="Cholesky" | custom-call | tf_op jit(solution)/shard_map/jit(cholesky)/cholesky | solution.py:50
  344.7 0.7 multiply_bitcast_fusion
  345.4 9.8 %custom-call.6 = f32[1,128,128]{1,2,0:T(8,128)S(1)} custom-call(f32[1,128,128]{2,1,0:T(8,128)S(1)} %get-tuple-element.89), custom_call_target="InvertDiagBlocksLowerTriangular" | custom-call | tf_op jit(solution)/shard_map/triangular_solve/custom-call.0 | solution.py:10
  355.2 3.5 convolution_bitcast_fusion.1
  358.7 2.4 fusion.32
  361.1 0.7 copy.19
  361.9 143.4 %all-reduce.8.cloned.1.call-done = f32[128,128]{0,1:T(8,128)} async-done(((f32[128,128]{0,1:T(8,128)}), f32[128,128]{0,1:T(8,128)}) %all-reduce.8.cloned.1.call-update) | async-done | bytes 65552 | tf_op jit(solution)/shard_map/psum | solution.py:52
  505.3 0.9 copy.17
  506.2 0.9 fusion.14
  507.1 11.9 %cholesky.55 = f32[128,128]{1,0:T(8,128)S(1)} custom-call(f32[128,128]{1,0:T(8,128)S(1)} %fusion.14), custom_call_target="Cholesky" | custom-call | tf_op jit(solution)/shard_map/jit(cholesky)/cholesky | solution.py:52
  519.0 0.7 compare_reduce_fusion
  519.8 2.3 convolution_multiply_fusion
  522.0 0.7 select_bitcast_fusion
  522.7 9.8 %custom-call.7 = f32[1,128,128]{1,2,0:T(8,128)S(1)} custom-call(f32[1,128,128]{2,1,0:T(8,128)S(1)} %select_bitcast_fusion), custom_call_target="InvertDiagBlocksLowerTriangular" | custom-call | tf_op jit(solution)/shard_map/triangular_solve/custom-call.0 | solution.py:10
  532.5 1.9 convolution_bitcast_fusion
  534.5 0.8 copy.18
  (49 shorter events, 4.3 us)
Async XLA Ops:
  7.2 1.0 copy-start
  7.2 171.2 %all-reduce.4.cloned.1.call-start = ((), (), s32[]{:S(2)}) async-start(), calls=%async_computation | async-start | bytes 4194304 | tf_op jit(solution)/shard_map/psum | solution.py:49
  79.6 250.9 %all-reduce.6.cloned.1.call-start = ((), (), s32[]{:S(2)}) async-start(), calls=%async_computation.1 | async-start | bytes 131072 | tf_op jit(solution)/shard_map/psum | solution.py:50
  184.7 320.6 %all-reduce.8.cloned.1.call-start = ((), (), s32[]{:S(2)}) async-start(), calls=%async_computation.2 | async-start | bytes 131072 | tf_op jit(solution)/shard_map/psum | solution.py:52
Sparse Core Ops, SparseCore 0:
  79.7 98.6 all-reduce.3
  184.8 145.6 all-reduce.5
  361.3 143.9 all-reduce.7
where the time goes:
time: 547 us; the launch traced here: 542 us
  waiting for transfers between devices  388 us (71%)
  matrix products  56.5 us (10%)
  other arithmetic  55.1 us (10%)
  local copies, waits for them, and re-layouts  27 us (5%)
  between operations  14.5 us (3%)
    psum x1, waiting for transfers between devices, per_device(): lower_one = jnp.linalg.cholesky(lax.psum(gram_of(sketch), 'user'))  146 us
    psum x1, waiting for transfers between devices, per_device(): lower_two = jnp.linalg.cholesky(lax.psum(gram_of(basis_one), 'user'))  143 us
    psum x1, waiting for transfers between devices, per_device(): sketch = lax.psum(partial_rows, 'item')  98.7 us
    dot_general x11, matrix products, turn(): jnp.einsum('sr,sik->rik', onehot, product, precision=lax.Precision.HIGHEST)  27.2 us
    another operation x3, other arithmetic, right_solve(): lax.linalg.triangular_solve(lower, rows, left_side=False, lower=True, tra...  20.3 us
    gather x11, local copies, waits for them, and re-layouts, turn(): chosen = blocks[placed[:, 1]]  20 us
    dot_general x11, matrix products, turn(): jnp.einsum('sij,sjk->sik', piece, chosen, preferred_element_type=jnp.floa...  12.8 us
    another operation x3, other arithmetic, per_device(): lower_two = jnp.linalg.cholesky(lax.psum(gram_of(basis_one), 'user'))  12.7 us
  transfers between devices with their start and end apart: 3, of which 3 were waited for; matrix products, arithmetic and copies ran while one was open for 0% of the time, Pallas kernels for 0%

commit v1 on v0

v1 whole, which is shorter than its diff:
```python
import jax
import jax.numpy as jnp
from jax import lax
from jax.experimental import pallas as pl
from jax.experimental.pallas import tpu as pltpu
from jax.sharding import Mesh, PartitionSpec as P

RB = 32
HALF = RB // 2
GROUP = 8
ROWS = "z", "y"
COLUMNS = "x", "core"
F32 = jnp.float32
HIGHEST = lax.Precision.HIGHEST
VMEM = pl.BlockSpec(memory_space=pltpu.VMEM)
SMEM = pl.BlockSpec(memory_space=pltpu.SMEM)
ANY = pl.BlockSpec(memory_space=pl.ANY)


def params(mib):
    return pltpu.CompilerParams(vmem_limit_bytes=mib * 2**20)


def mm(a, b, contract=(1, 0)):
    return lax.dot_general(
        a,
        b,
        (((contract[0],), (contract[1],)), ((), ())),
        precision=HIGHEST,
        preferred_element_type=F32,
    )


def two_sum(a, b):
    total = a + b
    other = total - a
    return total, (a - (total - other)) + (b - other)


def sketch_kernel(coords, count, core, tiles, omega, keep, give, held, products, total, fetched, sent):
    tile = held.shape[1]
    used = count[0, 0]
    groups = lax.div(used + (GROUP - 1), GROUP)
    mine = core[0]

    def fetch(g):
        part = pl.ds(pl.multiple_of(g * GROUP, GROUP), GROUP)
        return pltpu.make_async_copy(tiles.at[part], held.at[part], fetched.at[g])

    @pl.loop(0, groups)
    def _(g):
        fetch(g).start()

    total[...] = jnp.zeros_like(total)

    @pl.loop(0, groups)
    def _(g):
        fetch(g).wait()
        for u in range(GROUP):
            s = g * GROUP + u
            column = jnp.clip(coords[s, 1], 0, omega.shape[0] // tile - 1)
            block = omega[pl.ds(pl.multiple_of(column * tile, tile), tile), :]
            products[u] = jnp.dot(held[s], block, preferred_element_type=F32)
        for u in range(GROUP):
            s = g * GROUP + u
            row = coords[s, 0]
            x, rest = lax.div(row, 8), lax.rem(row, 8)
            other = (lax.div(rest, 4) != mine).astype(jnp.int32)
            place = other * HALF + x * 4 + lax.rem(rest, 4)
            place = jnp.where(s < used, jnp.clip(place, 0, RB - 1), RB)
            total[place] += products[u]

    out = [
        pltpu.make_async_copy(total.at[pl.ds(HALF, HALF)], give, sent.at[0]),
        pltpu.make_async_copy(total.at[pl.ds(0, HALF)], keep, sent.at[1]),
    ]
    for copy in out:
        copy.start()
    for copy in out:
        copy.wait()


def partial_sketch(tile_values, tile_coords, tile_counts, omega):
    slots, tile, _ = tile_values.shape
    width = omega.shape[1]
    half = jax.ShapeDtypeStruct((HALF, tile, width), F32)
    core = lax.axis_index("core").astype(jnp.int32).reshape(1)
    return pl.pallas_call(
        sketch_kernel,
        out_shape=(half, half),
        in_specs=[SMEM, SMEM, SMEM, ANY, VMEM],
        out_specs=(ANY, ANY),
        scratch_shapes=[
            pltpu.VMEM((slots, tile, tile), jnp.bfloat16),
            pltpu.VMEM((GROUP, tile, width), F32),
            pltpu.VMEM((RB + 1, tile, width), F32),
            pltpu.SemaphoreType.DMA((slots // GROUP,)),
            pltpu.SemaphoreType.DMA((2,)),
        ],
        compiler_params=params(32),
        name="sketch",
    )(tile_coords, tile_counts, core, tile_values, omega)


SLICES = 4
BITS = 8


def sliced(x, axis, count):
    grid = jnp.max(jnp.abs(x), axis=axis, keepdims=True) * (2.0**17)
    parts = []
    for _ in range(count):
        part = ((x + grid) - grid).astype(jnp.bfloat16)
        x = x - part.astype(F32)
        grid = grid * (2.0**-BITS)
        parts.append(part)
    return parts


def pair_of(orders):
    high, low = orders[0], jnp.zeros_like(orders[0])
    for term in orders[1:]:
        high, error = two_sum(high, term)
        low = low + error
    return two_sum(high, low)


def gram_kernel(pieces, sketch, pairs):
    rows, width = sketch.shape
    x = (pieces[0] + pieces[1]) + (pieces[2] + pieces[3])
    sketch[...] = x
    parts = sliced(x, 0, SLICES)
    across = jnp.concatenate(parts, axis=1)
    orders = [None] * (SLICES + 2)
    for i in range(SLICES):
        reach = min(SLICES, SLICES + 1 - i)
        block = lax.dot_general(
            parts[i],
            across[:, : reach * width],
            (((0,), (0,)), ((), ())),
            preferred_element_type=F32,
        )
        for j in range(reach):
            term = block[:, j * width : (j + 1) * width]
            o = i + j
            orders[o] = term if orders[o] is None else orders[o] + term
    high, low = pair_of([o for o in orders if o is not None])
    h = width // 2
    pairs[pl.ds(0, h, 4), :] = high[:h]
    pairs[pl.ds(1, h, 4), :] = high[h:]
    pairs[pl.ds(2, h, 4), :] = low[:h]
    pairs[pl.ds(3, h, 4), :] = low[h:]


def gram(pieces):
    _, rows, width = pieces.shape
    return pl.pallas_call(
        gram_kernel,
        out_shape=(
            jax.ShapeDtypeStruct((rows, width), F32),
            jax.ShapeDtypeStruct((2 * width, width), F32),
        ),
        in_specs=[VMEM],
        out_specs=(VMEM, VMEM),
        compiler_params=params(32),
        name="gram",
    )(pieces)


def add_kernel(given, summed):
    steps = given.shape[0] // 8
    total, error = given[0:8, :], jnp.zeros((8, given.shape[1]), F32)
    for k in range(1, steps):
        total, slip = two_sum(total, given[8 * k : 8 * k + 8, :])
        error = error + slip
    high, slip = two_sum(total[0:2], total[4:6])
    low = (error[0:2] + error[4:6]) + (total[2:4] + total[6:8]) + slip
    high, low = two_sum(high, low)
    chunk = jnp.concatenate([high, low, high, low], axis=0)
    for k in range(summed.shape[0] // 8):
        summed[8 * k : 8 * k + 8, :] = chunk


def add_pairs(given, copies):
    return pl.pallas_call(
        add_kernel,
        out_shape=jax.ShapeDtypeStruct((4 * copies, given.shape[1]), F32),
        in_specs=[VMEM],
        out_specs=VMEM,
        compiler_params=params(16),
        name="add_pairs",
    )(given)


PANEL = 8


def factor(rows):
    count = len(rows)
    width = PANEL * count
    place = lax.broadcasted_iota(jnp.int32, (PANEL, width), 0)
    lane = lax.broadcasted_iota(jnp.int32, (PANEL, width), 1)
    rows = list(rows)
    inverse = [(lane == place + PANEL * k).astype(F32) for k in range(count)]
    for k in range(count):
        a, x = rows[k], inverse[k]
        columns = [
            jnp.broadcast_to(a[:, PANEL * k + j : PANEL * k + j + 1], (PANEL, width)) for j in range(PANEL)
        ]
        scale = jnp.zeros((PANEL, width), F32)
        for j in range(PANEL):
            pivot = jnp.broadcast_to(columns[j][j : j + 1, :], (PANEL, width))
            root = lax.rsqrt(pivot)
            scale = jnp.where(place == j, root, scale)
            ratio = jnp.where(place > j, columns[j] * (root * root), 0.0)
            a = a - ratio * a[j : j + 1, :]
            x = x - ratio * x[j : j + 1, :]
            for l in range(j + 1, PANEL):
                columns[l] = columns[l] - ratio * columns[l][j : j + 1, :]
        a = jnp.where(lane >= place + PANEL * k, a * scale, 0.0)
        x = x * scale
        rows[k], inverse[k] = a, x
        if k + 1 < count:
            below = a[:, PANEL * (k + 1) :]
            change = mm(below, jnp.concatenate([a, x], axis=1), (0, 0))
            for i in range(k + 1, count):
                at = PANEL * (i - k - 1)
                rows[i] = rows[i] - change[at : at + PANEL, :width]
                inverse[i] = inverse[i] - change[at : at + PANEL, width:]
    return jnp.concatenate(rows, axis=0), jnp.concatenate(inverse, axis=0)


def panels(matrix):
    return [matrix[k : k + PANEL, :] for k in range(0, matrix.shape[0], PANEL)]


def finish_kernel(scale, pairs, sketch, basis, whole_r, one_r):
    width = sketch.shape[1]
    h = width // 2
    high = jnp.concatenate([pairs[pl.ds(0, h, 4), :], pairs[pl.ds(1, h, 4), :]], axis=0)
    low = jnp.concatenate([pairs[pl.ds(2, h, 4), :], pairs[pl.ds(3, h, 4), :]], axis=0)
    upper, inverse = factor(panels(high))
    parts = sliced(upper, 0, SLICES + 1)
    rest, carried = high, low
    for order in range(SLICES + 1):
        left = jnp.concatenate(parts[: order + 1], axis=0)
        right = jnp.concatenate(parts[: order + 1][::-1], axis=0)
        term = lax.dot_general(left, right, (((0,), (0,)), ((), ())), preferred_element_type=F32)
        rest, error = two_sum(rest, -term)
        carried = carried + error
    rest = rest + carried
    eye = lax.broadcasted_iota(jnp.int32, (width, width), 0) == lax.broadcasted_iota(
        jnp.int32, (width, width), 1
    )
    gram_two = mm(mm(inverse, rest), inverse, (1, 1)) + eye.astype(F32)
    upper_two, inverse_two = factor(panels(gram_two))
    both = mm(inverse_two, inverse)
    basis[...] = mm(sketch[...], both, (1, 1)) * scale[0]
    whole_r[...] = mm(upper_two, upper) / scale[0]
    one_r[...] = upper / scale[0]


def finish(pairs, sketch, scale):
    square = jax.ShapeDtypeStruct((sketch.shape[1],) * 2, F32)
    return pl.pallas_call(
        finish_kernel,
        out_shape=(jax.ShapeDtypeStruct(sketch.shape, F32), square, square),
        in_specs=[SMEM, VMEM, VMEM],
        out_specs=(VMEM, VMEM, VMEM),
        compiler_params=params(32),
        name="finish",
    )(scale.reshape(1), pairs, sketch)


def exchange(x, axes):
    return lax.all_to_all(x, axes, 0, 0, tiled=True)


def per_device(tile_values, tile_coords, tile_counts, omega):
    tile = tile_values.shape[2]
    width = omega.shape[1]
    keep, give = partial_sketch(tile_values, tile_coords, tile_counts, omega)
    got = lax.ppermute(give, "core", [(0, 1), (1, 0)])
    pieces = exchange(keep + got, "x")
    sketch, pairs = gram(pieces.reshape(4, HALF // 4 * tile, width))
    wide = ("y", "x", "core")
    pairs = add_pairs(exchange(pairs, wide), 8)
    pairs = add_pairs(exchange(pairs, "z"), 64)
    pairs = exchange(pairs, wide)
    total_rows = RB * tile * lax.axis_size(ROWS)
    return finish(pairs, sketch, jnp.sqrt(jnp.float32(total_rows)))


def solution(mesh):
    grid = Mesh(mesh.devices.reshape(8, 8, 4, 2), ("z", "y", "x", "core"))
    return jax.shard_map(
        per_device,
        mesh=grid,
        in_specs=(
            P(ROWS, COLUMNS, None),
            P(ROWS, COLUMNS),
            P(ROWS, COLUMNS),
            P(COLUMNS, None),
        ),
        out_specs=(P(ROWS + COLUMNS, None), P(), P()),
        check_vma=False,
    )
```

time: 547 us -> 108 us (0.20)
  waiting for transfers between devices: 388 us -> 2.26 us
  blocking collectives: 0 us -> 68.8 us
  matrix products: 56.5 us -> 0 us
  other arithmetic: 55.1 us -> 0.15 us
  local copies, waits for them, and re-layouts: 27 us -> 4.04 us
  Pallas kernels: 0 us -> 22.2 us
  between operations: 14.5 us -> 1.32 us
  starting transfers between devices: 0.3 us -> 8.79 us
    psum x3 -> x0, waiting for transfers between devices: 388 us -> none  [the longest x1 146 us: per_device(): lower_one = jnp.linalg.cholesky(lax.psum(gram_of(sketch), 'user'))]
    all_to_all x0 -> x4, blocking collectives: none -> 68.8 us  [exchange(): return lax.all_to_all(x, axes, 0, 0, tiled=True)]
    dot_general x25 -> x0, matrix products: 51 us -> none  [the longest x11 27.2 us: turn(): jnp.einsum('sr,sik->rik', onehot, product, precision=lax.Precision.HIGHEST)]
    another operation x9 -> x0, other arithmetic: 45.4 us -> none  [the longest x3 20.3 us: right_solve(): lax.linalg.triangular_solve(lower, rows, left_side=False, lower=True, tra...]
    pallas_call x0 -> x5, Pallas kernels: none -> 22.2 us  [the longest x1 18.6 us: finish(): pl.pallas_call(finish_kernel, out_shape=(jax.ShapeDtypeStruct(sketch.shap...]
    gather x11 -> x0, local copies, waits for them, and re-layouts: 20 us -> none  [turn(): chosen = blocks[placed[:, 1]]]
    ppermute x0 -> x1, starting transfers between devices: none -> 8.79 us  [per_device(): got = lax.ppermute(give, 'core', [(0, 1), (1, 0)])]
    convert_element_type x11 -> x0, other arithmetic: 7.17 us -> none  [turn(): ((slot_ids >= start_slot) & (slot_ids < stop_slot)).astype(jnp.float32)]
  transfers between devices with their start and end apart: 3 -> 1, of which waited for: 3 -> 1; matrix products, arithmetic and copies ran while one was open for 0% -> 0% of each run, Pallas kernels for 0% -> 0%
where the time goes in v1:
time: 108 us
  blocking collectives  68.8 us (64%)
  Pallas kernels  22.2 us (21%)
  starting transfers between devices  8.79 us (8%)
  local copies, waits for them, and re-layouts  4.04 us (4%)
  waiting for transfers between devices  2.26 us (2%)
  between operations  1.32 us (1%)
    all_to_all x4, blocking collectives, exchange(): return lax.all_to_all(x, axes, 0, 0, tiled=True)  68.8 us
    pallas_call x1, Pallas kernels, finish(): pl.pallas_call(finish_kernel, out_shape=(jax.ShapeDtypeStruct(sketch.shap...  18.6 us
    ppermute x1, starting transfers between devices, per_device(): got = lax.ppermute(give, 'core', [(0, 1), (1, 0)])  8.79 us
    unnamed x5, local copies, waits for them, and re-layouts  4.04 us
    pallas_call x1, Pallas kernels, partial_sketch(): pl.pallas_call(sketch_kernel, out_shape=(half, half), in_specs=[SMEM, SME...  2.96 us
    ppermute x1, waiting for transfers between devices, per_device(): got = lax.ppermute(give, 'core', [(0, 1), (1, 0)])  2.26 us
  transfers between devices with their start and end apart: 1, of which 1 were waited for; matrix products, arithmetic and copies ran while one was open for 0% of the time, Pallas kernels for 0%

profile of v1, /device:TPU:1, one launch (start us, length us, event | category | flops | bytes accessed | tf_op | source)
XLA Modules:
  0.0 107.6 jit_solution(3633363747466135311)
XLA Ops:
  1.3 0.8 copy.7.coords
  2.1 0.0 copy-start
  2.1 2.0 %copy-done = bf16[112,128,128]{2,1,0:T(8,128)(2,1)S(1)} copy-done((bf16[112,128,128]{2,1,0:T(8,128)(2,1)S(1)}, bf16[112,128,128]{2,1,0:T(8,128)(2,1)}, u32[]{:S(2)}) %copy-start) | copy-done | bytes 3670040
  4.1 0.0 copy-start.1
  4.1 1.2 %copy-done.1 = bf16[4096,128]{1,0:T(8,128)(2,1)S(1)} copy-done((bf16[4096,128]{1,0:T(8,128)(2,1)S(1)}, bf16[4096,128]{1,0:T(8,128)(2,1)}, u32[]{:S(2)}) %copy-start.1) | copy-done | bytes 1048600
  5.3 3.0 %sketch.1 = (f32[16,128,128]{2,1,0:T(8,128)S(1)}, f32[16,128,128]{2,1,0:T(8,128)S(1)}) custom-call(s32[112,2]{1,0:T(8,128)S(1)} %copy.7.coords, s32[1,1]{1,0:T(1,128)S(6)} %copy.8.count, s32[1]{0:T(128)} %bitcast.core, bf16[112,128,128]{2,1,0:T(8,128)(2,1)S(1)} %copy-done, bf16[4096,128]{1,0:T(8,128)(2,1)S(1)} %copy-done.1), custom_call_target="tpu_custom_call" | custom-call | tf_op jit(solution)/shard_map/sketch/pallas_call | solution.py:88
  8.3 8.8 %collective-permute-start = (f32[16,128,128]{2,1,0:T(8,128)S(1)}, f32[16,128,128]{2,1,0:T(8,128)S(1)}, u32[]{:S(2)}, u32[]{:S(2)}) collective-permute-start(f32[16,128,128]{2,1,0:T(8,128)S(1)} %get-tuple-element.8), channel_id=1, source_target_pairs={{0,1},{1,0},{2,3},{3,2},{4,5},{5,4},{6,7},{7,6},{8,9},{9,8},{10,11... | collective-permute-start | bytes 3145736 | tf_op jit(solution)/shard_map/ppermute | solution.py:283
  17.1 2.3 %collective-permute-done = f32[16,128,128]{2,1,0:T(8,128)S(1)} collective-permute-done((f32[16,128,128]{2,1,0:T(8,128)S(1)}, f32[16,128,128]{2,1,0:T(8,128)S(1)}, u32[]{:S(2)}, u32[]{:S(2)}) %collective-permute-start) | collective-permute-done | bytes 1048608 | tf_op jit(solution)/shard_map/ppermute | solution.py:283
  19.4 0.2 add.3
  19.5 17.3 %all_to_all.38 = f32[16,128,128]{2,1,0:T(8,128)S(1)} all-to-all(f32[16,128,128]{2,1,0:T(8,128)S(1)} %add.3), channel_id=1, replica_groups=mesh['z'=8,'y'=8,'x'=4,'core'=2] {'x'}, dimensions={0} | all-to-all | bytes 2097152 | tf_op jit(solution)/shard_map/all_to_all | solution.py:276
  36.8 0.6 gram.1
  37.4 17.7 %all_to_all.39 = f32[64,4,128]{2,1,0:T(4,128)S(1)} all-to-all(f32[64,4,128]{2,1,0:T(4,128)S(1)} %bitcast.12), channel_id=1, replica_groups=mesh['z'=8,'y'=8,'x'=4,'core'=2] {'y','x','core'}, dimensions={0} | all-to-all | bytes 262144 | tf_op jit(solution)/shard_map/all_to_all | solution.py:276
  55.0 0.1 add_pairs.2
  55.1 17.5 %all_to_all.40 = f32[8,4,128]{2,1,0:T(4,128)S(1)} all-to-all(f32[8,4,128]{2,1,0:T(4,128)S(1)} %bitcast.13), channel_id=1, replica_groups=mesh['z'=8,'y'=8,'x'=4,'core'=2] {'z'}, dimensions={0} | all-to-all | bytes 32768 | tf_op jit(solution)/shard_map/all_to_all | solution.py:276
  72.6 16.4 %all_to_all.41 = f32[64,4,128]{2,1,0:T(4,128)S(1)} all-to-all(f32[64,4,128]{2,1,0:T(4,128)S(1)} %bitcast.11), channel_id=1, replica_groups=mesh['z'=8,'y'=8,'x'=4,'core'=2] {'y','x','core'}, dimensions={0} | all-to-all | bytes 262144 | tf_op jit(solution)/shard_map/all_to_all | solution.py:276
  89.0 18.6 %finish.1 = (f32[512,128]{1,0:T(8,128)}, f32[128,128]{1,0:T(8,128)}, f32[128,128]{1,0:T(8,128)}) custom-call(f32[1]{0:T(128)} %constant.2.clone.1.scale, f32[256,128]{1,0:T(8,128)S(1)} %bitcast.9, f32[512,128]{1,0:T(8,128)S(1)} %get-tuple-element.10.sketch), custom_call_target="tpu_custom_call" | custom-call | tf_op jit(solution)/shard_map/finish/pallas_call | solution.py:265
  (1 shorter events, 0.0 us)
Async XLA Ops:
  2.1 2.0 %copy-start = (bf16[112,128,128]{2,1,0:T(8,128)(2,1)S(1)}, bf16[112,128,128]{2,1,0:T(8,128)(2,1)}, u32[]{:S(2)}) copy-start(bf16[112,128,128]{2,1,0:T(8,128)(2,1)} %tiles.1) | copy-start | bytes 11010052
  4.1 1.2 %copy-start.1 = (bf16[4096,128]{1,0:T(8,128)(2,1)S(1)}, bf16[4096,128]{1,0:T(8,128)(2,1)}, u32[]{:S(2)}) copy-start(bf16[4096,128]{1,0:T(8,128)(2,1)} %omega.1) | copy-start | bytes 3145732
  8.3 11.1 %collective-permute-start = (f32[16,128,128]{2,1,0:T(8,128)S(1)}, f32[16,128,128]{2,1,0:T(8,128)S(1)}, u32[]{:S(2)}, u32[]{:S(2)}) collective-permute-start(f32[16,128,128]{2,1,0:T(8,128)S(1)} %get-tuple-element.8), channel_id=1, source_target_pairs={{0,1},{1,0},{2,3},{3,2},{4,5},{5,4},{6,7},{7,6},{8,9},{9,8},{10,11... | collective-permute-start | bytes 3145736 | tf_op jit(solution)/shard_map/ppermute | solution.py:283

commit v2 on v1

v2 whole, which is shorter than its diff:
```python
import jax
import jax.numpy as jnp
from jax import lax
from jax.experimental import pallas as pl
from jax.experimental.pallas import tpu as pltpu
from jax.sharding import Mesh, PartitionSpec as P

RB = 32
HALF = RB // 2
PANEL = 8
GROUP = 8
ROWS = "z", "y"
COLUMNS = "x", "core"
F32 = jnp.float32
HIGHEST = lax.Precision.HIGHEST
VMEM = pl.BlockSpec(memory_space=pltpu.VMEM)
SMEM = pl.BlockSpec(memory_space=pltpu.SMEM)
HBM = pl.BlockSpec(memory_space=pltpu.HBM)


def params(mib):
    return pltpu.CompilerParams(vmem_limit_bytes=mib * 2**20)


def mm(a, b, contract=(1, 0)):
    return lax.dot_general(
        a,
        b,
        (((contract[0],), (contract[1],)), ((), ())),
        precision=HIGHEST,
        preferred_element_type=F32,
    )


def two_sum(a, b):
    total = a + b
    other = total - a
    return total, (a - (total - other)) + (b - other)


def sketch_kernel(coords, count, core, tiles, omega, total, held, blocks, products, fetched, ready):
    tile = held.shape[1]
    used = count[0, 0]
    groups = lax.div(used + (GROUP - 1), GROUP)
    mine = core[0]

    def fetch(g):
        part = pl.ds(pl.multiple_of(g * GROUP, GROUP), GROUP)
        return pltpu.make_async_copy(tiles.at[part], held.at[part], fetched.at[g])

    whole = pltpu.make_async_copy(omega, blocks, ready.at[0])
    whole.start()

    @pl.loop(0, groups)
    def _(g):
        fetch(g).start()

    total[...] = jnp.zeros_like(total)
    whole.wait()

    @pl.loop(0, groups)
    def _(g):
        fetch(g).wait()
        for u in range(GROUP):
            s = g * GROUP + u
            column = jnp.clip(coords[1, s], 0, blocks.shape[0] // tile - 1)
            block = blocks[pl.ds(pl.multiple_of(column * tile, tile), tile), :]
            products[u] = jnp.dot(held[s], block, preferred_element_type=F32)
        for u in range(GROUP):
            s = g * GROUP + u
            row = coords[0, s]
            x, rest = lax.div(row, 8), lax.rem(row, 8)
            own = (lax.div(rest, 4) == mine).astype(jnp.int32)
            place = own * HALF + x * 4 + lax.rem(rest, 4)
            place = jnp.where(s < used, jnp.clip(place, 0, RB - 1), RB)
            total[place] += products[u]


def partial_sketch(tile_values, tile_coords, tile_counts, omega):
    slots, tile, _ = tile_values.shape
    width = omega.shape[1]
    core = lax.axis_index("core").astype(jnp.int32).reshape(1)
    return pl.pallas_call(
        sketch_kernel,
        out_shape=jax.ShapeDtypeStruct((RB + 1, tile, width), F32),
        in_specs=[SMEM, SMEM, SMEM, HBM, HBM],
        out_specs=VMEM,
        scratch_shapes=[
            pltpu.VMEM((slots, tile, tile), jnp.bfloat16),
            pltpu.VMEM(omega.shape, jnp.bfloat16),
            pltpu.VMEM((GROUP, tile, width), F32),
            pltpu.SemaphoreType.DMA((slots // GROUP,)),
            pltpu.SemaphoreType.DMA((1,)),
        ],
        compiler_params=params(32),
        name="sketch",
    )(
        pltpu.with_memory_space_constraint(tile_coords.T, pltpu.HBM),
        tile_counts,
        core,
        pltpu.with_memory_space_constraint(tile_values, pltpu.HBM),
        pltpu.with_memory_space_constraint(omega, pltpu.HBM),
    )


SLICES = 4
BITS = 8


def sliced(x, axis, count):
    grid = jnp.max(jnp.abs(x), axis=axis, keepdims=True) * (2.0**17)
    parts = []
    for _ in range(count):
        part = ((x + grid) - grid).astype(jnp.bfloat16)
        x = x - part.astype(F32)
        grid = grid * (2.0**-BITS)
        parts.append(part)
    return parts


def pair_of(orders):
    high, low = orders[0], jnp.zeros_like(orders[0])
    for term in orders[1:]:
        high, error = two_sum(high, term)
        low = low + error
    return two_sum(high, low)


def gram_kernel(pieces, sketch, pairs):
    rows, width = sketch.shape
    x = (pieces[0] + pieces[1]) + (pieces[2] + pieces[3])
    sketch[...] = x
    parts = sliced(x, 0, SLICES)
    across = jnp.concatenate(parts, axis=1)
    orders = [None] * (SLICES + 2)
    for i in range(SLICES):
        reach = min(SLICES, SLICES + 1 - i)
        block = lax.dot_general(
            parts[i],
            across[:, : reach * width],
            (((0,), (0,)), ((), ())),
            preferred_element_type=F32,
        )
        for j in range(reach):
            term = block[:, j * width : (j + 1) * width]
            o = i + j
            orders[o] = term if orders[o] is None else orders[o] + term
    high, low = pair_of([o for o in orders if o is not None])
    for k in range(width // PANEL):
        at = slice(PANEL * k, PANEL * (k + 1))
        pairs[2 * PANEL * k : 2 * PANEL * k + PANEL, :] = high[at]
        pairs[2 * PANEL * k + PANEL : 2 * PANEL * (k + 1), :] = low[at]


def gram(pieces):
    _, rows, width = pieces.shape
    return pl.pallas_call(
        gram_kernel,
        out_shape=(
            jax.ShapeDtypeStruct((rows, width), F32),
            jax.ShapeDtypeStruct((2 * width, width), F32),
        ),
        in_specs=[VMEM],
        out_specs=(VMEM, VMEM),
        compiler_params=params(32),
        name="gram",
    )(pieces)


def add_kernel(given, summed):
    high, low = given[0:PANEL, :], given[PANEL : 2 * PANEL, :]
    for k in range(2 * PANEL, given.shape[0], 2 * PANEL):
        high, error = two_sum(high, given[k : k + PANEL, :])
        low = low + (given[k + PANEL : k + 2 * PANEL, :] + error)
    high, low = two_sum(high, low)
    for k in range(0, summed.shape[0], 2 * PANEL):
        summed[k : k + PANEL, :] = high
        summed[k + PANEL : k + 2 * PANEL, :] = low


def add_pairs(given, copies):
    return pl.pallas_call(
        add_kernel,
        out_shape=jax.ShapeDtypeStruct((2 * PANEL * copies, given.shape[1]), F32),
        in_specs=[VMEM],
        out_specs=VMEM,
        compiler_params=params(16),
        name="add_pairs",
    )(given)


def eliminate(a, x, k):
    shape = a.shape
    place = lax.broadcasted_iota(jnp.int32, shape, 0)
    columns = [jnp.broadcast_to(a[:, PANEL * k + j : PANEL * k + j + 1], shape) for j in range(PANEL)]
    scale = jnp.zeros(shape, F32)
    for j in range(PANEL):
        root = lax.rsqrt(jnp.broadcast_to(columns[j][j : j + 1, :], shape))
        scale = jnp.where(place == j, root, scale)
        ratio = jnp.where(place > j, columns[j] * (root * root), 0.0)
        a = a - ratio * a[j : j + 1, :]
        x = x - ratio * x[j : j + 1, :]
        for l in range(j + 1, PANEL):
            columns[l] = columns[l] - ratio * columns[l][j : j + 1, :]
    return a, x, scale


def factor(matrix):
    width = matrix.shape[0]
    count = width // PANEL
    place = lax.broadcasted_iota(jnp.int32, (PANEL, width), 0)
    lane = lax.broadcasted_iota(jnp.int32, (PANEL, width), 1)
    rows = [matrix[PANEL * k : PANEL * (k + 1), :] for k in range(count)]
    inverse = [(lane == place + PANEL * k).astype(F32) for k in range(count)]
    for k in range(count):
        near = slice(k, k + 2)
        a, x, scale = eliminate(jnp.concatenate(rows[near], axis=0), jnp.concatenate(inverse[near], axis=0), k)
        if k + 1 < count:
            rows[k + 1], inverse[k + 1] = a[PANEL:], x[PANEL:]
        a = jnp.where(lane >= place + PANEL * k, a[:PANEL] * scale[:PANEL], 0.0)
        x = x[:PANEL] * scale[:PANEL]
        rows[k], inverse[k] = a, x
        if k + 2 < count:
            change = mm(a[:, PANEL * (k + 2) :], jnp.concatenate([a, x], axis=1), (0, 0))
            for i in range(k + 2, count):
                at = PANEL * (i - k - 2)
                rows[i] = rows[i] - change[at : at + PANEL, :width]
                inverse[i] = inverse[i] - change[at : at + PANEL, width:]
    return jnp.concatenate(rows, axis=0), jnp.concatenate(inverse, axis=0)


def mm3(a, b, contract=(1, 0)):
    a_high, b_high = a.astype(jnp.bfloat16), b.astype(jnp.bfloat16)
    a_low = (a - a_high.astype(F32)).astype(jnp.bfloat16)
    b_low = (b - b_high.astype(F32)).astype(jnp.bfloat16)
    return lax.dot_general(
        jnp.concatenate([a_high, a_high, a_low], axis=contract[0]),
        jnp.concatenate([b_high, b_low, b_high], axis=contract[1]),
        (((contract[0],), (contract[1],)), ((), ())),
        preferred_element_type=F32,
    )


def finish_kernel(scale, pairs, sketch, basis, whole_r, one_r, upper_two, change_two):
    width = sketch.shape[1]
    chunks = range(0, 2 * width, 2 * PANEL)
    high = jnp.concatenate([pairs[k : k + PANEL, :] for k in chunks], axis=0)
    low = jnp.concatenate([pairs[k + PANEL : k + 2 * PANEL, :] for k in chunks], axis=0)
    place = lax.broadcasted_iota(jnp.int32, (width, width), 0)
    lane = lax.broadcasted_iota(jnp.int32, (width, width), 1)
    eye = (place == lane).astype(F32)
    upper, inverse = factor(high)
    one_r[...] = upper / scale[0]
    inverse = inverse - mm3(mm(inverse, upper, (1, 1)) - eye, inverse)
    parts = sliced(upper, 0, SLICES + 1)
    rest, carried = high, low
    for order in range(SLICES + 1):
        left = jnp.concatenate(parts[: order + 1], axis=0)
        right = jnp.concatenate(parts[: order + 1][::-1], axis=0)
        term = lax.dot_general(left, right, (((0,), (0,)), ((), ())), preferred_element_type=F32)
        rest, error = two_sum(rest, -term)
        carried = carried + error
    rest = rest + carried
    excess = mm3(mm3(inverse, rest), inverse, (1, 1))
    weight = jnp.where(place > lane, 1.0, jnp.where(place == lane, 0.5, 0.0))
    left, change = excess, None
    for _ in range(2):
        half = left * weight
        square = mm3(half, half)
        outer = mm3(half, half, (1, 1))
        third = mm3(half, outer)
        change = -half if change is None else change - half - mm3(half, change)
        left = (third + third.T) - (square + square.T + outer)
    change_two[...] = change
    lower_two = excess + change.T + mm3(excess, change, (1, 1))
    upper_two[...] = jnp.where(place <= lane, lower_two.T, 0.0) + eye

    @pl.when(jnp.logical_not(jnp.max(jnp.abs(left)) < 1e-6))
    def _():
        upper_full, inverse_full = factor(excess + eye)
        upper_two[...] = upper_full
        change_two[...] = inverse_full - eye

    both = inverse + mm3(change_two[...], inverse)
    basis[...] = mm(sketch[...], both, (1, 1)) * scale[0]
    whole_r[...] = (upper + mm3(upper_two[...] - eye, upper)) / scale[0]


def finish(pairs, sketch, scale):
    square = jax.ShapeDtypeStruct((sketch.shape[1],) * 2, F32)
    return pl.pallas_call(
        finish_kernel,
        out_shape=(jax.ShapeDtypeStruct(sketch.shape, F32), square, square),
        in_specs=[SMEM, VMEM, VMEM],
        out_specs=(VMEM, VMEM, VMEM),
        scratch_shapes=[pltpu.VMEM(square.shape, F32), pltpu.VMEM(square.shape, F32)],
        compiler_params=params(32),
        name="finish",
    )(scale.reshape(1), pairs, sketch)


def exchange(x, axes):
    return lax.all_to_all(x, axes, 0, 0, tiled=True)


def per_device(tile_values, tile_coords, tile_counts, omega):
    tile = tile_values.shape[2]
    width = omega.shape[1]
    partial = partial_sketch(tile_values, tile_coords, tile_counts, omega)
    got = lax.ppermute(partial[:HALF], "core", [(0, 1), (1, 0)])
    pieces = exchange(partial[HALF:RB] + got, "x")
    sketch, pairs = gram(pieces.reshape(4, HALF // 4 * tile, width))
    near, far = ("y", "core"), ("z", "x")
    pairs = add_pairs(exchange(pairs, near), 32)
    pairs = add_pairs(exchange(pairs, far), 16)
    pairs = exchange(pairs, near)
    total_rows = RB * tile * lax.axis_size(ROWS)
    return finish(pairs, sketch, jnp.sqrt(jnp.float32(total_rows)))


def solution(mesh):
    grid = Mesh(mesh.devices.reshape(8, 8, 4, 2), ("z", "y", "x", "core"))
    return jax.shard_map(
        per_device,
        mesh=grid,
        in_specs=(
            P(ROWS, COLUMNS, None),
            P(ROWS, COLUMNS),
            P(ROWS, COLUMNS),
            P(COLUMNS, None),
        ),
        out_specs=(P(ROWS + COLUMNS, None), P(), P()),
        check_vma=False,
    )
```

time: 108 us -> 93.8 us (0.87)
  Pallas kernels: 22.2 us -> 12 us
  local copies, waits for them, and re-layouts: 4.04 us -> 0.08 us
    pallas_call x1, Pallas kernels: 18.6 us -> 8.32 us  [finish(): pl.pallas_call(finish_kernel, out_shape=(jax.ShapeDtypeStruct(sketch.shap...]
    unnamed x5 -> x0, local copies, waits for them, and re-layouts: 4.04 us -> none
where the time goes in v2:
time: 93.8 us; the launch traced here: 93.5 us
  blocking collectives  68 us (72%)
  Pallas kernels  12 us (13%)
  starting transfers between devices  9.74 us (10%)
  waiting for transfers between devices  2.26 us (2%)
  between operations  1.32 us (1%)
    all_to_all x4, blocking collectives, exchange(): return lax.all_to_all(x, axes, 0, 0, tiled=True)  68 us
    ppermute x1, starting transfers between devices, per_device(): got = lax.ppermute(partial[:HALF], 'core', [(0, 1), (1, 0)])  9.74 us
    pallas_call x1, Pallas kernels, finish(): pl.pallas_call(finish_kernel, out_shape=(jax.ShapeDtypeStruct(sketch.shap...  8.32 us
    pallas_call x1, Pallas kernels, partial_sketch(): pl.pallas_call(sketch_kernel, out_shape=jax.ShapeDtypeStruct((RB + 1, til...  3.02 us
    ppermute x1, waiting for transfers between devices, per_device(): got = lax.ppermute(partial[:HALF], 'core', [(0, 1), (1, 0)])  2.26 us
  transfers between devices with their start and end apart: 1, of which 1 were waited for; matrix products, arithmetic and copies ran while one was open for 0% of the time, Pallas kernels for 0%

profile of v2, /device:TPU:1, one launch (start us, length us, event | category | flops | bytes accessed | tf_op | source)
XLA Modules:
  0.0 93.5 jit_solution(15520906189863615323)
XLA Ops:
  1.3 3.0 %sketch.1 = f32[33,128,128]{2,1,0:T(8,128)S(1)} custom-call(s32[2,112]{1,0:T(2,128)} %bitcast.16, s32[1,1]{1,0:T(1,128)S(6)} %copy.7.count, s32[1]{0:T(128)} %bitcast.1.core, bf16[112,128,128]{2,1,0:T(8,128)(2,1)} %tiles.1, bf16[4096,128]{1,0:T(8,128)(2,1)} %omega.1), custom_call_target="tpu_custom_call" | custom-call | tf_op jit(solution)/shard_map/sketch/pallas_call | solution.py:83
  4.3 0.1 slice.9
  4.4 9.7 %collective-permute-start = (f32[16,128,128]{2,1,0:T(8,128)S(1)}, f32[16,128,128]{2,1,0:T(8,128)S(1)}, u32[]{:S(2)}, u32[]{:S(2)}) collective-permute-start(f32[16,128,128]{2,1,0:T(8,128)S(1)} %slice.9), channel_id=1, source_target_pairs={{0,1},{1,0},{2,3},{3,2},{4,5},{5,4},{6,7},{7,6},{8,9},{9,8},{10,11... | collective-permute-start | bytes 3145736 | tf_op jit(solution)/shard_map/ppermute | solution.py:310
  14.1 2.3 %collective-permute-done = f32[16,128,128]{2,1,0:T(8,128)S(1)} collective-permute-done((f32[16,128,128]{2,1,0:T(8,128)S(1)}, f32[16,128,128]{2,1,0:T(8,128)S(1)}, u32[]{:S(2)}, u32[]{:S(2)}) %collective-permute-start) | collective-permute-done | bytes 1048608 | tf_op jit(solution)/shard_map/ppermute | solution.py:310
  16.4 0.1 slice_add_fusion
  16.6 17.3 %all_to_all.38 = f32[16,128,128]{2,1,0:T(8,128)S(1)} all-to-all(f32[16,128,128]{2,1,0:T(8,128)S(1)} %slice_add_fusion), channel_id=1, replica_groups=mesh['z'=8,'y'=8,'x'=4,'core'=2] {'x'}, dimensions={0} | all-to-all | bytes 2097152 | tf_op jit(solution)/shard_map/all_to_all | solution.py:303
  33.8 0.6 gram.1
  34.4 13.0 %all_to_all.39 = f32[16,16,128]{2,1,0:T(8,128)S(1)} all-to-all(f32[16,16,128]{2,1,0:T(8,128)S(1)} %bitcast.15), channel_id=1, replica_groups=mesh['z'=8,'y'=8,'x'=4,'core'=2] {'y','core'}, dimensions={0} | all-to-all | bytes 262144 | tf_op jit(solution)/shard_map/all_to_all | solution.py:303
  47.5 24.5 %all_to_all.40 = f32[32,16,128]{2,1,0:T(8,128)S(1)} all-to-all(f32[32,16,128]{2,1,0:T(8,128)S(1)} %bitcast.10), channel_id=1, replica_groups=mesh['z'=8,'y'=8,'x'=4,'core'=2] {'z','x'}, dimensions={0} | all-to-all | bytes 524288 | tf_op jit(solution)/shard_map/all_to_all | solution.py:303
  72.0 0.1 add_pairs.3
  72.0 13.2 %all_to_all.41 = f32[16,16,128]{2,1,0:T(8,128)S(1)} all-to-all(f32[16,16,128]{2,1,0:T(8,128)S(1)} %bitcast.13), channel_id=1, replica_groups=mesh['z'=8,'y'=8,'x'=4,'core'=2] {'y','core'}, dimensions={0} | all-to-all | bytes 262144 | tf_op jit(solution)/shard_map/all_to_all | solution.py:303
  85.2 8.3 %finish.1 = (f32[512,128]{1,0:T(8,128)}, f32[128,128]{1,0:T(8,128)}, f32[128,128]{1,0:T(8,128)}) custom-call(f32[1]{0:T(128)} %constant.2.clone.1.scale, f32[256,128]{1,0:T(8,128)S(1)} %bitcast.14, f32[512,128]{1,0:T(8,128)S(1)} %get-tuple-element.6.sketch), custom_call_target="tpu_custom_call" | custom-call | tf_op jit(solution)/shard_map/finish/pallas_call | solution.py:291
  (1 shorter events, 0.0 us)
Async XLA Ops:
  4.4 12.0 %collective-permute-start = (f32[16,128,128]{2,1,0:T(8,128)S(1)}, f32[16,128,128]{2,1,0:T(8,128)S(1)}, u32[]{:S(2)}, u32[]{:S(2)}) collective-permute-start(f32[16,128,128]{2,1,0:T(8,128)S(1)} %slice.9), channel_id=1, source_target_pairs={{0,1},{1,0},{2,3},{3,2},{4,5},{5,4},{6,7},{7,6},{8,9},{9,8},{10,11... | collective-permute-start | bytes 3145736 | tf_op jit(solution)/shard_map/ppermute | solution.py:310

commit v3 on v2

--- a/solution.py
+++ b/solution.py
@@ -8,7 +8,8 @@
 RB = 32
 HALF = RB // 2
 PANEL = 8
-GROUP = 8
+AHEAD = 3
+GROUP = 28
 ROWS = "z", "y"
 COLUMNS = "x", "core"
 F32 = jnp.float32
@@ -213,20 +214,42 @@
     rows = [matrix[PANEL * k : PANEL * (k + 1), :] for k in range(count)]
     inverse = [(lane == place + PANEL * k).astype(F32) for k in range(count)]
     for k in range(count):
-        near = slice(k, k + 2)
-        a, x, scale = eliminate(jnp.concatenate(rows[near], axis=0), jnp.concatenate(inverse[near], axis=0), k)
-        if k + 1 < count:
-            rows[k + 1], inverse[k + 1] = a[PANEL:], x[PANEL:]
-        a = jnp.where(lane >= place + PANEL * k, a[:PANEL] * scale[:PANEL], 0.0)
-        x = x[:PANEL] * scale[:PANEL]
-        rows[k], inverse[k] = a, x
-        if k + 2 < count:
-            change = mm(a[:, PANEL * (k + 2) :], jnp.concatenate([a, x], axis=1), (0, 0))
-            for i in range(k + 2, count):
-                at = PANEL * (i - k - 2)
-                rows[i] = rows[i] - change[at : at + PANEL, :width]
-                inverse[i] = inverse[i] - change[at : at + PANEL, width:]
+        near = range(k, min(k + AHEAD, count))
+        a, x, scale = eliminate(
+            jnp.concatenate([rows[i] for i in near], axis=0),
+            jnp.concatenate([inverse[i] for i in near], axis=0),
+            k,
+        )
+        for i in near:
+            at = slice(PANEL * (i - k), PANEL * (i - k + 1))
+            rows[i], inverse[i] = a[at], x[at]
+        rows[k] = jnp.where(lane >= place + PANEL * k, rows[k] * scale[:PANEL], 0.0)
+        inverse[k] = inverse[k] * scale[:PANEL]
+        if k + AHEAD < count:
+            change = outer(rows[k], jnp.concatenate([rows[k], inverse[k]], axis=1))
+            for i in range(k + AHEAD, count):
+                at = slice(PANEL * i, PANEL * (i + 1))
+                rows[i] = rows[i] - change[at, :width]
+                inverse[i] = inverse[i] - change[at, width:]
     return jnp.concatenate(rows, axis=0), jnp.concatenate(inverse, axis=0)
+
+
+def thirds(x):
+    high = x.astype(jnp.bfloat16).astype(F32)
+    rest = x - high
+    middle = rest.astype(jnp.bfloat16).astype(F32)
+    return high, middle, rest - middle
+
+
+def outer(a, b):
+    ah, am, al = thirds(a)
+    bh, bm, bl = thirds(b)
+    return lax.dot_general(
+        jnp.concatenate([ah, ah, am, ah, am, al], axis=0).astype(jnp.bfloat16),
+        jnp.concatenate([bh, bm, bh, bl, bm, bh], axis=0).astype(jnp.bfloat16),
+        (((0,), (0,)), ((), ())),
+        preferred_element_type=F32,
+    )
 
 
 def mm3(a, b, contract=(1, 0)):
@@ -267,10 +290,10 @@
     for _ in range(2):
         half = left * weight
         square = mm3(half, half)
-        outer = mm3(half, half, (1, 1))
-        third = mm3(half, outer)
+        sides = mm3(half, half, (1, 1))
+        third = mm3(half, sides)
         change = -half if change is None else change - half - mm3(half, change)
-        left = (third + third.T) - (square + square.T + outer)
+        left = (third + third.T) - (square + square.T + sides)
     change_two[...] = change
     lower_two = excess + change.T + mm3(excess, change, (1, 1))
     upper_two[...] = jnp.where(place <= lane, lower_two.T, 0.0) + eye

time: 93.8 us -> 91.6 us (0.977)
  Pallas kernels: 12 us -> 10.3 us
    pallas_call x1, Pallas kernels: 8.32 us -> 6.87 us  [finish(): pl.pallas_call(finish_kernel, out_shape=(jax.ShapeDtypeStruct(sketch.shap...]
where the time goes in v3:
time: 91.6 us; the launch traced here: 91.3 us
  blocking collectives  67.9 us (74%)
  Pallas kernels  10.3 us (11%)
  starting transfers between devices  9.3 us (10%)
  waiting for transfers between devices  2.26 us (2%)
  between operations  1.32 us (1%)
    all_to_all x4, blocking collectives, exchange(): return lax.all_to_all(x, axes, 0, 0, tiled=True)  67.9 us
    ppermute x1, starting transfers between devices, per_device(): got = lax.ppermute(partial[:HALF], 'core', [(0, 1), (1, 0)])  9.3 us
    pallas_call x1, Pallas kernels, finish(): pl.pallas_call(finish_kernel, out_shape=(jax.ShapeDtypeStruct(sketch.shap...  6.87 us
    pallas_call x1, Pallas kernels, partial_sketch(): pl.pallas_call(sketch_kernel, out_shape=jax.ShapeDtypeStruct((RB + 1, til...  2.73 us
    ppermute x1, waiting for transfers between devices, per_device(): got = lax.ppermute(partial[:HALF], 'core', [(0, 1), (1, 0)])  2.26 us
  transfers between devices with their start and end apart: 1, of which 1 were waited for; matrix products, arithmetic and copies ran while one was open for 0% of the time, Pallas kernels for 0%

profile of v3, /device:TPU:1, one launch (start us, length us, event | category | flops | bytes accessed | tf_op | source)
XLA Modules:
  0.0 91.3 jit_solution(3685956875399416323)
XLA Ops:
  1.3 2.7 %sketch.1 = f32[33,128,128]{2,1,0:T(8,128)S(1)} custom-call(s32[2,112]{1,0:T(2,128)} %bitcast.16, s32[1,1]{1,0:T(1,128)S(6)} %copy.7.count, s32[1]{0:T(128)} %bitcast.1.core, bf16[112,128,128]{2,1,0:T(8,128)(2,1)} %tiles.1, bf16[4096,128]{1,0:T(8,128)(2,1)} %omega.1), custom_call_target="tpu_custom_call" | custom-call | tf_op jit(solution)/shard_map/sketch/pallas_call | solution.py:84
  4.0 0.1 slice.9
  4.1 9.3 %collective-permute-start = (f32[16,128,128]{2,1,0:T(8,128)S(1)}, f32[16,128,128]{2,1,0:T(8,128)S(1)}, u32[]{:S(2)}, u32[]{:S(2)}) collective-permute-start(f32[16,128,128]{2,1,0:T(8,128)S(1)} %slice.9), channel_id=1, source_target_pairs={{0,1},{1,0},{2,3},{3,2},{4,5},{5,4},{6,7},{7,6},{8,9},{9,8},{10,11... | collective-permute-start | bytes 3145736 | tf_op jit(solution)/shard_map/ppermute | solution.py:333
  13.4 2.3 %collective-permute-done = f32[16,128,128]{2,1,0:T(8,128)S(1)} collective-permute-done((f32[16,128,128]{2,1,0:T(8,128)S(1)}, f32[16,128,128]{2,1,0:T(8,128)S(1)}, u32[]{:S(2)}, u32[]{:S(2)}) %collective-permute-start) | collective-permute-done | bytes 1048608 | tf_op jit(solution)/shard_map/ppermute | solution.py:333
  15.7 0.1 slice_add_fusion
  15.8 17.3 %all_to_all.38 = f32[16,128,128]{2,1,0:T(8,128)S(1)} all-to-all(f32[16,128,128]{2,1,0:T(8,128)S(1)} %slice_add_fusion), channel_id=1, replica_groups=mesh['z'=8,'y'=8,'x'=4,'core'=2] {'x'}, dimensions={0} | all-to-all | bytes 2097152 | tf_op jit(solution)/shard_map/all_to_all | solution.py:326
  33.1 0.6 gram.1
  33.7 14.3 %all_to_all.39 = f32[16,16,128]{2,1,0:T(8,128)S(1)} all-to-all(f32[16,16,128]{2,1,0:T(8,128)S(1)} %bitcast.15), channel_id=1, replica_groups=mesh['z'=8,'y'=8,'x'=4,'core'=2] {'y','core'}, dimensions={0} | all-to-all | bytes 262144 | tf_op jit(solution)/shard_map/all_to_all | solution.py:326
  48.0 23.1 %all_to_all.40 = f32[32,16,128]{2,1,0:T(8,128)S(1)} all-to-all(f32[32,16,128]{2,1,0:T(8,128)S(1)} %bitcast.10), channel_id=1, replica_groups=mesh['z'=8,'y'=8,'x'=4,'core'=2] {'z','x'}, dimensions={0} | all-to-all | bytes 524288 | tf_op jit(solution)/shard_map/all_to_all | solution.py:326
  71.2 0.1 add_pairs.3
  71.2 13.2 %all_to_all.41 = f32[16,16,128]{2,1,0:T(8,128)S(1)} all-to-all(f32[16,16,128]{2,1,0:T(8,128)S(1)} %bitcast.13), channel_id=1, replica_groups=mesh['z'=8,'y'=8,'x'=4,'core'=2] {'y','core'}, dimensions={0} | all-to-all | bytes 262144 | tf_op jit(solution)/shard_map/all_to_all | solution.py:326
  84.4 6.9 %finish.1 = (f32[512,128]{1,0:T(8,128)}, f32[128,128]{1,0:T(8,128)}, f32[128,128]{1,0:T(8,128)}) custom-call(f32[1]{0:T(128)} %constant.2.clone.1.scale, f32[256,128]{1,0:T(8,128)S(1)} %bitcast.14, f32[512,128]{1,0:T(8,128)S(1)} %get-tuple-element.6.sketch), custom_call_target="tpu_custom_call" | custom-call | tf_op jit(solution)/shard_map/finish/pallas_call | solution.py:314
  (1 shorter events, 0.0 us)
Async XLA Ops:
  4.1 11.6 %collective-permute-start = (f32[16,128,128]{2,1,0:T(8,128)S(1)}, f32[16,128,128]{2,1,0:T(8,128)S(1)}, u32[]{:S(2)}, u32[]{:S(2)}) collective-permute-start(f32[16,128,128]{2,1,0:T(8,128)S(1)} %slice.9), channel_id=1, source_target_pairs={{0,1},{1,0},{2,3},{3,2},{4,5},{5,4},{6,7},{7,6},{8,9},{9,8},{10,11... | collective-permute-start | bytes 3145736 | tf_op jit(solution)/shard_map/ppermute | solution.py:333

commit v4 on v3

--- a/solution.py
+++ b/solution.py
@@ -190,41 +190,43 @@
     )(given)
 
 
-def eliminate(a, x, k):
-    shape = a.shape
-    place = lax.broadcasted_iota(jnp.int32, shape, 0)
-    columns = [jnp.broadcast_to(a[:, PANEL * k + j : PANEL * k + j + 1], shape) for j in range(PANEL)]
-    scale = jnp.zeros(shape, F32)
-    for j in range(PANEL):
-        root = lax.rsqrt(jnp.broadcast_to(columns[j][j : j + 1, :], shape))
-        scale = jnp.where(place == j, root, scale)
-        ratio = jnp.where(place > j, columns[j] * (root * root), 0.0)
-        a = a - ratio * a[j : j + 1, :]
-        x = x - ratio * x[j : j + 1, :]
-        for l in range(j + 1, PANEL):
-            columns[l] = columns[l] - ratio * columns[l][j : j + 1, :]
-    return a, x, scale
+def spread(rows, at):
+    return [jnp.broadcast_to(rows[:, at + j : at + j + 1], rows.shape) for j in range(PANEL)]
 
 
 def factor(matrix):
     width = matrix.shape[0]
     count = width // PANEL
-    place = lax.broadcasted_iota(jnp.int32, (PANEL, width), 0)
-    lane = lax.broadcasted_iota(jnp.int32, (PANEL, width), 1)
+    shape = (PANEL, width)
+    place = lax.broadcasted_iota(jnp.int32, shape, 0)
+    lane = lax.broadcasted_iota(jnp.int32, shape, 1)
     rows = [matrix[PANEL * k : PANEL * (k + 1), :] for k in range(count)]
     inverse = [(lane == place + PANEL * k).astype(F32) for k in range(count)]
+    columns = {}
     for k in range(count):
         near = range(k, min(k + AHEAD, count))
-        a, x, scale = eliminate(
-            jnp.concatenate([rows[i] for i in near], axis=0),
-            jnp.concatenate([inverse[i] for i in near], axis=0),
-            k,
-        )
         for i in near:
-            at = slice(PANEL * (i - k), PANEL * (i - k + 1))
-            rows[i], inverse[i] = a[at], x[at]
-        rows[k] = jnp.where(lane >= place + PANEL * k, rows[k] * scale[:PANEL], 0.0)
-        inverse[k] = inverse[k] * scale[:PANEL]
+            if i not in columns:
+                columns[i] = spread(rows[i], PANEL * k)
+        later = {i: spread(rows[i], PANEL * (k + 1)) if k + 1 < count else [] for i in near}
+        scale = jnp.zeros(shape, F32)
+        for j in range(PANEL):
+            root = lax.rsqrt(jnp.broadcast_to(columns[k][j][j : j + 1, :], shape))
+            scale = jnp.where(place == j, root, scale)
+            ratio = {i: columns[i][j] * (root * root) for i in near}
+            ratio[k] = jnp.where(place > j, ratio[k], 0.0)
+            row, unit = rows[k][j : j + 1, :], inverse[k][j : j + 1, :]
+            now = [c[j : j + 1, :] for c in columns[k]]
+            next_ = [c[j : j + 1, :] for c in later[k]]
+            for i in near:
+                rows[i] = rows[i] - ratio[i] * row
+                inverse[i] = inverse[i] - ratio[i] * unit
+                for l in range(j + 1, PANEL):
+                    columns[i][l] = columns[i][l] - ratio[i] * now[l]
+                later[i] = [c - ratio[i] * d for c, d in zip(later[i], next_)]
+        rows[k] = jnp.where(lane >= place + PANEL * k, rows[k] * scale, 0.0)
+        inverse[k] = inverse[k] * scale
+        columns = {i: later[i] for i in near if i > k}
         if k + AHEAD < count:
             change = outer(rows[k], jnp.concatenate([rows[k], inverse[k]], axis=1))
             for i in range(k + AHEAD, count):
@@ -274,7 +276,8 @@
     eye = (place == lane).astype(F32)
     upper, inverse = factor(high)
     one_r[...] = upper / scale[0]
-    inverse = inverse - mm3(mm(inverse, upper, (1, 1)) - eye, inverse)
+    basis_one = mm(sketch[...], inverse, (1, 1))
+    flaw = mm(inverse, upper, (1, 1)) - eye
     parts = sliced(upper, 0, SLICES + 1)
     rest, carried = high, low
     for order in range(SLICES + 1):
@@ -284,29 +287,28 @@
         rest, error = two_sum(rest, -term)
         carried = carried + error
     rest = rest + carried
-    excess = mm3(mm3(inverse, rest), inverse, (1, 1))
+    excess = mm3(mm3(inverse, rest), inverse, (1, 1)) + (flaw + flaw.T + mm3(flaw, flaw, (1, 1)))
     weight = jnp.where(place > lane, 1.0, jnp.where(place == lane, 0.5, 0.0))
-    left, change = excess, None
-    for _ in range(2):
-        half = left * weight
-        square = mm3(half, half)
-        sides = mm3(half, half, (1, 1))
-        third = mm3(half, sides)
-        change = -half if change is None else change - half - mm3(half, change)
-        left = (third + third.T) - (square + square.T + sides)
+    half = excess * weight
+    square = mm3(half, half)
+    sides = mm3(half, half, (1, 1))
+    third = mm3(half, sides)
+    left = (third + third.T) - (square + square.T + sides)
+    last = left * weight
+    change = mm3(last, half) - (half + last)
     change_two[...] = change
     lower_two = excess + change.T + mm3(excess, change, (1, 1))
-    upper_two[...] = jnp.where(place <= lane, lower_two.T, 0.0) + eye
-
-    @pl.when(jnp.logical_not(jnp.max(jnp.abs(left)) < 1e-6))
+    upper_two[...] = jnp.where(place <= lane, lower_two.T, 0.0)
+
+    @pl.when(jnp.logical_not(jnp.sum(last * last) < 3e-7))
     def _():
         upper_full, inverse_full = factor(excess + eye)
-        upper_two[...] = upper_full
+        upper_two[...] = upper_full - eye
         change_two[...] = inverse_full - eye
 
-    both = inverse + mm3(change_two[...], inverse)
-    basis[...] = mm(sketch[...], both, (1, 1)) * scale[0]
-    whole_r[...] = (upper + mm3(upper_two[...] - eye, upper)) / scale[0]
+    basis[...] = (basis_one + mm3(basis_one, change_two[...], (1, 1))) * scale[0]
+    upper = upper - mm3(flaw, upper - mm3(flaw, upper, (0, 0)), (0, 0))
+    whole_r[...] = (upper + mm3(upper_two[...], upper)) / scale[0]
 
 
 def finish(pairs, sketch, scale):

time: 91.6 us -> 90.4 us (0.987)
  starting transfers between devices: 9.3 us -> 7.76 us
    ppermute x1, starting transfers between devices: 9.3 us -> 7.76 us  [per_device(): got = lax.ppermute(partial[:HALF], 'core', [(0, 1), (1, 0)])]
    pallas_call x1, Pallas kernels: 2.73 us -> 3.76 us  [partial_sketch(): pl.pallas_call(sketch_kernel, out_shape=jax.ShapeDtypeStruct((RB + 1, til...]
where the time goes in v4:
time: 90.4 us; the launch traced here: 90 us
  blocking collectives  68.1 us (75%)
  Pallas kernels  10.4 us (12%)
  starting transfers between devices  7.76 us (9%)
  waiting for transfers between devices  2.26 us (2%)
  between operations  1.32 us (1%)
    all_to_all x4, blocking collectives, exchange(): return lax.all_to_all(x, axes, 0, 0, tiled=True)  68.1 us
    ppermute x1, starting transfers between devices, per_device(): got = lax.ppermute(partial[:HALF], 'core', [(0, 1), (1, 0)])  7.76 us
    pallas_call x1, Pallas kernels, finish(): pl.pallas_call(finish_kernel, out_shape=(jax.ShapeDtypeStruct(sketch.shap...  5.98 us
    pallas_call x1, Pallas kernels, partial_sketch(): pl.pallas_call(sketch_kernel, out_shape=jax.ShapeDtypeStruct((RB + 1, til...  3.76 us
    ppermute x1, waiting for transfers between devices, per_device(): got = lax.ppermute(partial[:HALF], 'core', [(0, 1), (1, 0)])  2.26 us
  transfers between devices with their start and end apart: 1, of which 1 were waited for; matrix products, arithmetic and copies ran while one was open for 0% of the time, Pallas kernels for 0%

profile of v4, /device:TPU:1, one launch (start us, length us, event | category | flops | bytes accessed | tf_op | source)
XLA Modules:
  0.0 90.0 jit_solution(12795444136123804102)
XLA Ops:
  1.3 3.8 %sketch.1 = f32[33,128,128]{2,1,0:T(8,128)S(1)} custom-call(s32[2,112]{1,0:T(2,128)} %bitcast.16, s32[1,1]{1,0:T(1,128)S(6)} %copy.7.count, s32[1]{0:T(128)} %bitcast.1.core, bf16[112,128,128]{2,1,0:T(8,128)(2,1)} %tiles.1, bf16[4096,128]{1,0:T(8,128)(2,1)} %omega.1), custom_call_target="tpu_custom_call" | custom-call | tf_op jit(solution)/shard_map/sketch/pallas_call | solution.py:84
  5.0 0.1 slice.9
  5.1 7.8 %collective-permute-start = (f32[16,128,128]{2,1,0:T(8,128)S(1)}, f32[16,128,128]{2,1,0:T(8,128)S(1)}, u32[]{:S(2)}, u32[]{:S(2)}) collective-permute-start(f32[16,128,128]{2,1,0:T(8,128)S(1)} %slice.9), channel_id=1, source_target_pairs={{0,1},{1,0},{2,3},{3,2},{4,5},{5,4},{6,7},{7,6},{8,9},{9,8},{10,11... | collective-permute-start | bytes 3145736 | tf_op jit(solution)/shard_map/ppermute | solution.py:335
  12.9 2.3 %collective-permute-done = f32[16,128,128]{2,1,0:T(8,128)S(1)} collective-permute-done((f32[16,128,128]{2,1,0:T(8,128)S(1)}, f32[16,128,128]{2,1,0:T(8,128)S(1)}, u32[]{:S(2)}, u32[]{:S(2)}) %collective-permute-start) | collective-permute-done | bytes 1048608 | tf_op jit(solution)/shard_map/ppermute | solution.py:335
  15.2 0.1 slice_add_fusion
  15.3 17.3 %all_to_all.38 = f32[16,128,128]{2,1,0:T(8,128)S(1)} all-to-all(f32[16,128,128]{2,1,0:T(8,128)S(1)} %slice_add_fusion), channel_id=1, replica_groups=mesh['z'=8,'y'=8,'x'=4,'core'=2] {'x'}, dimensions={0} | all-to-all | bytes 2097152 | tf_op jit(solution)/shard_map/all_to_all | solution.py:328
  32.6 0.6 gram.1
  33.2 13.5 %all_to_all.39 = f32[16,16,128]{2,1,0:T(8,128)S(1)} all-to-all(f32[16,16,128]{2,1,0:T(8,128)S(1)} %bitcast.15), channel_id=1, replica_groups=mesh['z'=8,'y'=8,'x'=4,'core'=2] {'y','core'}, dimensions={0} | all-to-all | bytes 262144 | tf_op jit(solution)/shard_map/all_to_all | solution.py:328
  46.7 24.1 %all_to_all.40 = f32[32,16,128]{2,1,0:T(8,128)S(1)} all-to-all(f32[32,16,128]{2,1,0:T(8,128)S(1)} %bitcast.10), channel_id=1, replica_groups=mesh['z'=8,'y'=8,'x'=4,'core'=2] {'z','x'}, dimensions={0} | all-to-all | bytes 524288 | tf_op jit(solution)/shard_map/all_to_all | solution.py:328
  70.8 0.1 add_pairs.3
  70.9 13.2 %all_to_all.41 = f32[16,16,128]{2,1,0:T(8,128)S(1)} all-to-all(f32[16,16,128]{2,1,0:T(8,128)S(1)} %bitcast.13), channel_id=1, replica_groups=mesh['z'=8,'y'=8,'x'=4,'core'=2] {'y','core'}, dimensions={0} | all-to-all | bytes 262144 | tf_op jit(solution)/shard_map/all_to_all | solution.py:328
  84.1 6.0 %finish.1 = (f32[512,128]{1,0:T(8,128)}, f32[128,128]{1,0:T(8,128)}, f32[128,128]{1,0:T(8,128)}) custom-call(f32[1]{0:T(128)} %constant.2.clone.1.scale, f32[256,128]{1,0:T(8,128)S(1)} %bitcast.14, f32[512,128]{1,0:T(8,128)S(1)} %get-tuple-element.6.sketch), custom_call_target="tpu_custom_call" | custom-call | tf_op jit(solution)/shard_map/finish/pallas_call | solution.py:316
  (1 shorter events, 0.0 us)
Async XLA Ops:
  5.1 10.0 %collective-permute-start = (f32[16,128,128]{2,1,0:T(8,128)S(1)}, f32[16,128,128]{2,1,0:T(8,128)S(1)}, u32[]{:S(2)}, u32[]{:S(2)}) collective-permute-start(f32[16,128,128]{2,1,0:T(8,128)S(1)} %slice.9), channel_id=1, source_target_pairs={{0,1},{1,0},{2,3},{3,2},{4,5},{5,4},{6,7},{7,6},{8,9},{9,8},{10,11... | collective-permute-start | bytes 3145736 | tf_op jit(solution)/shard_map/ppermute | solution.py:335

commit v5 on v4

--- a/solution.py
+++ b/solution.py
@@ -7,6 +7,7 @@
 
 RB = 32
 HALF = RB // 2
+CHUNK = 4
 PANEL = 8
 AHEAD = 3
 GROUP = 28
@@ -147,10 +148,9 @@
             o = i + j
             orders[o] = term if orders[o] is None else orders[o] + term
     high, low = pair_of([o for o in orders if o is not None])
-    for k in range(width // PANEL):
-        at = slice(PANEL * k, PANEL * (k + 1))
-        pairs[2 * PANEL * k : 2 * PANEL * k + PANEL, :] = high[at]
-        pairs[2 * PANEL * k + PANEL : 2 * PANEL * (k + 1), :] = low[at]
+    for k in range(width // CHUNK):
+        at = slice(CHUNK * k, CHUNK * (k + 1))
+        pairs[2 * CHUNK * k : 2 * CHUNK * (k + 1), :] = jnp.concatenate([high[at], low[at]], axis=0)
 
 
 def gram(pieces):
@@ -169,20 +169,21 @@
 
 
 def add_kernel(given, summed):
-    high, low = given[0:PANEL, :], given[PANEL : 2 * PANEL, :]
-    for k in range(2 * PANEL, given.shape[0], 2 * PANEL):
-        high, error = two_sum(high, given[k : k + PANEL, :])
-        low = low + (given[k + PANEL : k + 2 * PANEL, :] + error)
-    high, low = two_sum(high, low)
-    for k in range(0, summed.shape[0], 2 * PANEL):
-        summed[k : k + PANEL, :] = high
-        summed[k + PANEL : k + 2 * PANEL, :] = low
+    step = 2 * CHUNK
+    total, error = given[0:step, :], jnp.zeros((step, given.shape[1]), F32)
+    for k in range(step, given.shape[0], step):
+        total, slip = two_sum(total, given[k : k + step, :])
+        error = error + slip
+    high, low = two_sum(total[:CHUNK], total[CHUNK:] + error[:CHUNK])
+    chunk = jnp.concatenate([high, low], axis=0)
+    for k in range(0, summed.shape[0], step):
+        summed[k : k + step, :] = chunk
 
 
 def add_pairs(given, copies):
     return pl.pallas_call(
         add_kernel,
-        out_shape=jax.ShapeDtypeStruct((2 * PANEL * copies, given.shape[1]), F32),
+        out_shape=jax.ShapeDtypeStruct((2 * CHUNK * copies, given.shape[1]), F32),
         in_specs=[VMEM],
         out_specs=VMEM,
         compiler_params=params(16),
@@ -268,9 +269,9 @@
 
 def finish_kernel(scale, pairs, sketch, basis, whole_r, one_r, upper_two, change_two):
     width = sketch.shape[1]
-    chunks = range(0, 2 * width, 2 * PANEL)
-    high = jnp.concatenate([pairs[k : k + PANEL, :] for k in chunks], axis=0)
-    low = jnp.concatenate([pairs[k + PANEL : k + 2 * PANEL, :] for k in chunks], axis=0)
+    chunks = [pairs[k : k + 2 * CHUNK, :] for k in range(0, 2 * width, 2 * CHUNK)]
+    high = jnp.concatenate([c[:CHUNK] for c in chunks], axis=0)
+    low = jnp.concatenate([c[CHUNK:] for c in chunks], axis=0)
     place = lax.broadcasted_iota(jnp.int32, (width, width), 0)
     lane = lax.broadcasted_iota(jnp.int32, (width, width), 1)
     eye = (place == lane).astype(F32)
@@ -335,9 +336,9 @@
     got = lax.ppermute(partial[:HALF], "core", [(0, 1), (1, 0)])
     pieces = exchange(partial[HALF:RB] + got, "x")
     sketch, pairs = gram(pieces.reshape(4, HALF // 4 * tile, width))
-    near, far = ("y", "core"), ("z", "x")
-    pairs = add_pairs(exchange(pairs, near), 32)
-    pairs = add_pairs(exchange(pairs, far), 16)
+    near, far = ("y", "x"), ("z", "core")
+    pairs = add_pairs(exchange(pairs, near), 16)
+    pairs = add_pairs(exchange(pairs, far), 32)
     pairs = exchange(pairs, near)
     total_rows = RB * tile * lax.axis_size(ROWS)
     return finish(pairs, sketch, jnp.sqrt(jnp.float32(total_rows)))

time: 90.4 us -> 87.2 us (0.965)
  blocking collectives: 68.1 us -> 64.9 us
    all_to_all x4, blocking collectives: 68.1 us -> 64.9 us  [exchange(): return lax.all_to_all(x, axes, 0, 0, tiled=True)]
where the time goes in v5:
time: 87.2 us; the launch traced here: 86.8 us
  blocking collectives  64.9 us (74%)
  Pallas kernels  9.91 us (11%)
  starting transfers between devices  8.28 us (9%)
  waiting for transfers between devices  2.26 us (3%)
  between operations  1.32 us (2%)
    all_to_all x4, blocking collectives, exchange(): return lax.all_to_all(x, axes, 0, 0, tiled=True)  64.9 us
    ppermute x1, starting transfers between devices, per_device(): got = lax.ppermute(partial[:HALF], 'core', [(0, 1), (1, 0)])  8.28 us
    pallas_call x1, Pallas kernels, finish(): pl.pallas_call(finish_kernel, out_shape=(jax.ShapeDtypeStruct(sketch.shap...  5.98 us
    pallas_call x1, Pallas kernels, partial_sketch(): pl.pallas_call(sketch_kernel, out_shape=jax.ShapeDtypeStruct((RB + 1, til...  3.25 us
    ppermute x1, waiting for transfers between devices, per_device(): got = lax.ppermute(partial[:HALF], 'core', [(0, 1), (1, 0)])  2.26 us
  transfers between devices with their start and end apart: 1, of which 1 were waited for; matrix products, arithmetic and copies ran while one was open for 0% of the time, Pallas kernels for 0%

profile of v5, /device:TPU:1, one launch (start us, length us, event | category | flops | bytes accessed | tf_op | source)
XLA Modules:
  0.0 86.8 jit_solution(14270819763251117246)
XLA Ops:
  1.3 3.2 %sketch.1 = f32[33,128,128]{2,1,0:T(8,128)S(1)} custom-call(s32[2,112]{1,0:T(2,128)} %bitcast.16, s32[1,1]{1,0:T(1,128)S(6)} %copy.7.count, s32[1]{0:T(128)} %bitcast.1.core, bf16[112,128,128]{2,1,0:T(8,128)(2,1)} %tiles.1, bf16[4096,128]{1,0:T(8,128)(2,1)} %omega.1), custom_call_target="tpu_custom_call" | custom-call | tf_op jit(solution)/shard_map/sketch/pallas_call | solution.py:85
  4.5 0.1 slice.9
  4.6 8.3 %collective-permute-start = (f32[16,128,128]{2,1,0:T(8,128)S(1)}, f32[16,128,128]{2,1,0:T(8,128)S(1)}, u32[]{:S(2)}, u32[]{:S(2)}) collective-permute-start(f32[16,128,128]{2,1,0:T(8,128)S(1)} %slice.9), channel_id=1, source_target_pairs={{0,1},{1,0},{2,3},{3,2},{4,5},{5,4},{6,7},{7,6},{8,9},{9,8},{10,11... | collective-permute-start | bytes 3145736 | tf_op jit(solution)/shard_map/ppermute | solution.py:336
  12.9 2.3 %collective-permute-done = f32[16,128,128]{2,1,0:T(8,128)S(1)} collective-permute-done((f32[16,128,128]{2,1,0:T(8,128)S(1)}, f32[16,128,128]{2,1,0:T(8,128)S(1)}, u32[]{:S(2)}, u32[]{:S(2)}) %collective-permute-start) | collective-permute-done | bytes 1048608 | tf_op jit(solution)/shard_map/ppermute | solution.py:336
  15.2 0.1 slice_add_fusion
  15.3 17.3 %all_to_all.38 = f32[16,128,128]{2,1,0:T(8,128)S(1)} all-to-all(f32[16,128,128]{2,1,0:T(8,128)S(1)} %slice_add_fusion), channel_id=1, replica_groups=mesh['z'=8,'y'=8,'x'=4,'core'=2] {'x'}, dimensions={0} | all-to-all | bytes 2097152 | tf_op jit(solution)/shard_map/all_to_all | solution.py:329
  32.6 0.6 gram.1
  33.2 13.2 %all_to_all.39 = f32[32,8,128]{2,1,0:T(8,128)S(1)} all-to-all(f32[32,8,128]{2,1,0:T(8,128)S(1)} %bitcast.15), channel_id=1, replica_groups=mesh['z'=8,'y'=8,'x'=4,'core'=2] {'y','x'}, dimensions={0} | all-to-all | bytes 262144 | tf_op jit(solution)/shard_map/all_to_all | solution.py:329
  46.4 0.1 add_pairs.2
  46.5 21.6 %all_to_all.40 = f32[16,8,128]{2,1,0:T(8,128)S(1)} all-to-all(f32[16,8,128]{2,1,0:T(8,128)S(1)} %bitcast.13), channel_id=1, replica_groups=mesh['z'=8,'y'=8,'x'=4,'core'=2] {'z','core'}, dimensions={0} | all-to-all | bytes 131072 | tf_op jit(solution)/shard_map/all_to_all | solution.py:329
  68.1 12.8 %all_to_all.41 = f32[32,8,128]{2,1,0:T(8,128)S(1)} all-to-all(f32[32,8,128]{2,1,0:T(8,128)S(1)} %bitcast.12), channel_id=1, replica_groups=mesh['z'=8,'y'=8,'x'=4,'core'=2] {'y','x'}, dimensions={0} | all-to-all | bytes 262144 | tf_op jit(solution)/shard_map/all_to_all | solution.py:329
  80.9 6.0 %finish.1 = (f32[512,128]{1,0:T(8,128)}, f32[128,128]{1,0:T(8,128)}, f32[128,128]{1,0:T(8,128)}) custom-call(f32[1]{0:T(128)} %constant.2.clone.1.scale, f32[256,128]{1,0:T(8,128)S(1)} %bitcast.10, f32[512,128]{1,0:T(8,128)S(1)} %get-tuple-element.6.sketch), custom_call_target="tpu_custom_call" | custom-call | tf_op jit(solution)/shard_map/finish/pallas_call | solution.py:317
  (1 shorter events, 0.0 us)
Async XLA Ops:
  4.6 10.5 %collective-permute-start = (f32[16,128,128]{2,1,0:T(8,128)S(1)}, f32[16,128,128]{2,1,0:T(8,128)S(1)}, u32[]{:S(2)}, u32[]{:S(2)}) collective-permute-start(f32[16,128,128]{2,1,0:T(8,128)S(1)} %slice.9), channel_id=1, source_target_pairs={{0,1},{1,0},{2,3},{3,2},{4,5},{5,4},{6,7},{7,6},{8,9},{9,8},{10,11... | collective-permute-start | bytes 3145736 | tf_op jit(solution)/shard_map/ppermute | solution.py:336

commit v6 on v5

--- a/solution.py
+++ b/solution.py
@@ -1,3 +1,6 @@
+import functools
+import math
+
 import jax
 import jax.numpy as jnp
 from jax import lax
@@ -40,25 +43,30 @@
     return total, (a - (total - other)) + (b - other)
 
 
-def sketch_kernel(coords, count, core, tiles, omega, total, held, blocks, products, fetched, ready):
+def sketch_kernel(count, places, tiles, omega, total, held, blocks, products, coords, fetched, ready):
     tile = held.shape[1]
     used = count[0, 0]
     groups = lax.div(used + (GROUP - 1), GROUP)
-    mine = core[0]
+    mine = lax.axis_index("core")
 
     def fetch(g):
         part = pl.ds(pl.multiple_of(g * GROUP, GROUP), GROUP)
         return pltpu.make_async_copy(tiles.at[part], held.at[part], fetched.at[g])
 
-    whole = pltpu.make_async_copy(omega, blocks, ready.at[0])
-    whole.start()
+    first = [
+        pltpu.make_async_copy(places, coords, ready.at[0]),
+        pltpu.make_async_copy(omega, blocks, ready.at[1]),
+    ]
+    for copy in first:
+        copy.start()
 
     @pl.loop(0, groups)
     def _(g):
         fetch(g).start()
 
     total[...] = jnp.zeros_like(total)
-    whole.wait()
+    for copy in first:
+        copy.wait()
 
     @pl.loop(0, groups)
     def _(g):
@@ -81,25 +89,24 @@
 def partial_sketch(tile_values, tile_coords, tile_counts, omega):
     slots, tile, _ = tile_values.shape
     width = omega.shape[1]
-    core = lax.axis_index("core").astype(jnp.int32).reshape(1)
     return pl.pallas_call(
         sketch_kernel,
         out_shape=jax.ShapeDtypeStruct((RB + 1, tile, width), F32),
-        in_specs=[SMEM, SMEM, SMEM, HBM, HBM],
+        in_specs=[SMEM, HBM, HBM, HBM],
         out_specs=VMEM,
         scratch_shapes=[
             pltpu.VMEM((slots, tile, tile), jnp.bfloat16),
             pltpu.VMEM(omega.shape, jnp.bfloat16),
             pltpu.VMEM((GROUP, tile, width), F32),
+            pltpu.SMEM((2, slots), jnp.int32),
             pltpu.SemaphoreType.DMA((slots // GROUP,)),
-            pltpu.SemaphoreType.DMA((1,)),
+            pltpu.SemaphoreType.DMA((2,)),
         ],
         compiler_params=params(32),
         name="sketch",
     )(
+        tile_counts,
         pltpu.with_memory_space_constraint(tile_coords.T, pltpu.HBM),
-        tile_counts,
-        core,
         pltpu.with_memory_space_constraint(tile_values, pltpu.HBM),
         pltpu.with_memory_space_constraint(omega, pltpu.HBM),
     )
@@ -276,7 +283,7 @@
     lane = lax.broadcasted_iota(jnp.int32, (width, width), 1)
     eye = (place == lane).astype(F32)
     upper, inverse = factor(high)
-    one_r[...] = upper / scale[0]
+    one_r[...] = upper / scale
     basis_one = mm(sketch[...], inverse, (1, 1))
     flaw = mm(inverse, upper, (1, 1)) - eye
     parts = sliced(upper, 0, SLICES + 1)
@@ -307,22 +314,22 @@
         upper_two[...] = upper_full - eye
         change_two[...] = inverse_full - eye
 
-    basis[...] = (basis_one + mm3(basis_one, change_two[...], (1, 1))) * scale[0]
+    basis[...] = (basis_one + mm3(basis_one, change_two[...], (1, 1))) * scale
     upper = upper - mm3(flaw, upper - mm3(flaw, upper, (0, 0)), (0, 0))
-    whole_r[...] = (upper + mm3(upper_two[...], upper)) / scale[0]
+    whole_r[...] = (upper + mm3(upper_two[...], upper)) / scale
 
 
 def finish(pairs, sketch, scale):
     square = jax.ShapeDtypeStruct((sketch.shape[1],) * 2, F32)
     return pl.pallas_call(
-        finish_kernel,
+        functools.partial(finish_kernel, scale),
         out_shape=(jax.ShapeDtypeStruct(sketch.shape, F32), square, square),
-        in_specs=[SMEM, VMEM, VMEM],
+        in_specs=[VMEM, VMEM],
         out_specs=(VMEM, VMEM, VMEM),
         scratch_shapes=[pltpu.VMEM(square.shape, F32), pltpu.VMEM(square.shape, F32)],
         compiler_params=params(32),
         name="finish",
-    )(scale.reshape(1), pairs, sketch)
+    )(pairs, sketch)
 
 
 def exchange(x, axes):
@@ -341,7 +348,7 @@
     pairs = add_pairs(exchange(pairs, far), 32)
     pairs = exchange(pairs, near)
     total_rows = RB * tile * lax.axis_size(ROWS)
-    return finish(pairs, sketch, jnp.sqrt(jnp.float32(total_rows)))
+    return finish(pairs, sketch, math.sqrt(total_rows))
 
 
 def solution(mesh):

time: 87.2 us -> 86.6 us (level)
  starting transfers between devices: 8.28 us -> 7.27 us
    ppermute x1, starting transfers between devices: 8.28 us -> 7.27 us  [per_device(): got = lax.ppermute(partial[:HALF], 'core', [(0, 1), (1, 0)])]
where the time goes in v6:
time: 86.6 us; the launch traced here: 86.3 us
  blocking collectives  65 us (75%)
  Pallas kernels  10.2 us (12%)
  starting transfers between devices  7.27 us (8%)
  waiting for transfers between devices  2.26 us (3%)
  between operations  1.32 us (2%)
    all_to_all x4, blocking collectives, exchange(): return lax.all_to_all(x, axes, 0, 0, tiled=True)  65 us
    ppermute x1, starting transfers between devices, per_device(): got = lax.ppermute(partial[:HALF], 'core', [(0, 1), (1, 0)])  7.27 us
    pallas_call x1, Pallas kernels, finish(): pl.pallas_call(functools.partial(finish_kernel, scale), out_shape=(jax.Sh...  5.99 us
    pallas_call x1, Pallas kernels, partial_sketch(): pl.pallas_call(sketch_kernel, out_shape=jax.ShapeDtypeStruct((RB + 1, til...  3.58 us
    ppermute x1, waiting for transfers between devices, per_device(): got = lax.ppermute(partial[:HALF], 'core', [(0, 1), (1, 0)])  2.26 us
  transfers between devices with their start and end apart: 1, of which 1 were waited for; matrix products, arithmetic and copies ran while one was open for 0% of the time, Pallas kernels for 0%

profile of v6, /device:TPU:1, one launch (start us, length us, event | category | flops | bytes accessed | tf_op | source)
XLA Modules:
  0.0 86.3 jit_solution(15895831709582264639)
XLA Ops:
  1.3 3.6 %sketch.1 = f32[33,128,128]{2,1,0:T(8,128)S(1)} custom-call(s32[1,1]{1,0:T(1,128)S(6)} %copy.7.count, s32[2,112]{1,0:T(2,128)} %bitcast.15, bf16[112,128,128]{2,1,0:T(8,128)(2,1)} %tiles.1, bf16[4096,128]{1,0:T(8,128)(2,1)} %omega.1), custom_call_target="tpu_custom_call" | custom-call | tf_op jit(solution)/shard_map/sketch/pallas_call | solution.py:92
  4.9 0.1 slice.9
  5.0 7.3 %collective-permute-start = (f32[16,128,128]{2,1,0:T(8,128)S(1)}, f32[16,128,128]{2,1,0:T(8,128)S(1)}, u32[]{:S(2)}, u32[]{:S(2)}) collective-permute-start(f32[16,128,128]{2,1,0:T(8,128)S(1)} %slice.9), channel_id=1, source_target_pairs={{0,1},{1,0},{2,3},{3,2},{4,5},{5,4},{6,7},{7,6},{8,9},{9,8},{10,11... | collective-permute-start | bytes 3145736 | tf_op jit(solution)/shard_map/ppermute | solution.py:343
  12.2 2.3 %collective-permute-done = f32[16,128,128]{2,1,0:T(8,128)S(1)} collective-permute-done((f32[16,128,128]{2,1,0:T(8,128)S(1)}, f32[16,128,128]{2,1,0:T(8,128)S(1)}, u32[]{:S(2)}, u32[]{:S(2)}) %collective-permute-start) | collective-permute-done | bytes 1048608 | tf_op jit(solution)/shard_map/ppermute | solution.py:343
  14.5 0.1 slice_add_fusion
  14.6 17.3 %all_to_all.38 = f32[16,128,128]{2,1,0:T(8,128)S(1)} all-to-all(f32[16,128,128]{2,1,0:T(8,128)S(1)} %slice_add_fusion), channel_id=1, replica_groups=mesh['z'=8,'y'=8,'x'=4,'core'=2] {'x'}, dimensions={0} | all-to-all | bytes 2097152 | tf_op jit(solution)/shard_map/all_to_all | solution.py:336
  31.9 0.6 gram.1
  32.5 12.7 %all_to_all.39 = f32[32,8,128]{2,1,0:T(8,128)S(1)} all-to-all(f32[32,8,128]{2,1,0:T(8,128)S(1)} %bitcast.14), channel_id=1, replica_groups=mesh['z'=8,'y'=8,'x'=4,'core'=2] {'y','x'}, dimensions={0} | all-to-all | bytes 262144 | tf_op jit(solution)/shard_map/all_to_all | solution.py:336
  45.2 0.1 add_pairs.2
  45.2 22.2 %all_to_all.40 = f32[16,8,128]{2,1,0:T(8,128)S(1)} all-to-all(f32[16,8,128]{2,1,0:T(8,128)S(1)} %bitcast.12), channel_id=1, replica_groups=mesh['z'=8,'y'=8,'x'=4,'core'=2] {'z','core'}, dimensions={0} | all-to-all | bytes 131072 | tf_op jit(solution)/shard_map/all_to_all | solution.py:336
  67.5 12.9 %all_to_all.41 = f32[32,8,128]{2,1,0:T(8,128)S(1)} all-to-all(f32[32,8,128]{2,1,0:T(8,128)S(1)} %bitcast.11), channel_id=1, replica_groups=mesh['z'=8,'y'=8,'x'=4,'core'=2] {'y','x'}, dimensions={0} | all-to-all | bytes 262144 | tf_op jit(solution)/shard_map/all_to_all | solution.py:336
  80.3 6.0 %finish.1 = (f32[512,128]{1,0:T(8,128)}, f32[128,128]{1,0:T(8,128)}, f32[128,128]{1,0:T(8,128)}) custom-call(f32[256,128]{1,0:T(8,128)S(1)} %bitcast.9, f32[512,128]{1,0:T(8,128)S(1)} %get-tuple-element.6.sketch), custom_call_target="tpu_custom_call" | custom-call | tf_op jit(solution)/shard_map/finish/pallas_call | solution.py:324
  (1 shorter events, 0.0 us)
Async XLA Ops:
  5.0 9.5 %collective-permute-start = (f32[16,128,128]{2,1,0:T(8,128)S(1)}, f32[16,128,128]{2,1,0:T(8,128)S(1)}, u32[]{:S(2)}, u32[]{:S(2)}) collective-permute-start(f32[16,128,128]{2,1,0:T(8,128)S(1)} %slice.9), channel_id=1, source_target_pairs={{0,1},{1,0},{2,3},{3,2},{4,5},{5,4},{6,7},{7,6},{8,9},{9,8},{10,11... | collective-permute-start | bytes 3145736 | tf_op jit(solution)/shard_map/ppermute | solution.py:343

commit v7 on v6

--- a/solution.py
+++ b/solution.py
@@ -274,7 +274,7 @@
     )
 
 
-def finish_kernel(scale, pairs, sketch, basis, whole_r, one_r, upper_two, change_two):
+def finish_kernel(scale, pairs, sketch, basis, whole_r, one_r):
     width = sketch.shape[1]
     chunks = [pairs[k : k + 2 * CHUNK, :] for k in range(0, 2 * width, 2 * CHUNK)]
     high = jnp.concatenate([c[:CHUNK] for c in chunks], axis=0)
@@ -283,7 +283,7 @@
     lane = lax.broadcasted_iota(jnp.int32, (width, width), 1)
     eye = (place == lane).astype(F32)
     upper, inverse = factor(high)
-    one_r[...] = upper / scale
+    one_r[...] = upper * (1.0 / scale)
     basis_one = mm(sketch[...], inverse, (1, 1))
     flaw = mm(inverse, upper, (1, 1)) - eye
     parts = sliced(upper, 0, SLICES + 1)
@@ -304,19 +304,20 @@
     left = (third + third.T) - (square + square.T + sides)
     last = left * weight
     change = mm3(last, half) - (half + last)
-    change_two[...] = change
     lower_two = excess + change.T + mm3(excess, change, (1, 1))
-    upper_two[...] = jnp.where(place <= lane, lower_two.T, 0.0)
+    upper_two = jnp.where(place <= lane, lower_two.T, 0.0)
+    upper = upper - mm3(flaw, upper - mm3(flaw, upper, (0, 0)), (0, 0))
+
+    def store(upper_two, change):
+        basis[...] = (basis_one + mm3(basis_one, change, (1, 1))) * scale
+        whole_r[...] = (upper + mm3(upper_two, upper)) * (1.0 / scale)
+
+    store(upper_two, change)
 
     @pl.when(jnp.logical_not(jnp.sum(last * last) < 3e-7))
     def _():
         upper_full, inverse_full = factor(excess + eye)
-        upper_two[...] = upper_full - eye
-        change_two[...] = inverse_full - eye
-
-    basis[...] = (basis_one + mm3(basis_one, change_two[...], (1, 1))) * scale
-    upper = upper - mm3(flaw, upper - mm3(flaw, upper, (0, 0)), (0, 0))
-    whole_r[...] = (upper + mm3(upper_two[...], upper)) / scale
+        store(upper_full - eye, inverse_full - eye)
 
 
 def finish(pairs, sketch, scale):
@@ -326,7 +327,6 @@
         out_shape=(jax.ShapeDtypeStruct(sketch.shape, F32), square, square),
         in_specs=[VMEM, VMEM],
         out_specs=(VMEM, VMEM, VMEM),
-        scratch_shapes=[pltpu.VMEM(square.shape, F32), pltpu.VMEM(square.shape, F32)],
         compiler_params=params(32),
         name="finish",
     )(pairs, sketch)
@@ -343,7 +343,7 @@
     got = lax.ppermute(partial[:HALF], "core", [(0, 1), (1, 0)])
     pieces = exchange(partial[HALF:RB] + got, "x")
     sketch, pairs = gram(pieces.reshape(4, HALF // 4 * tile, width))
-    near, far = ("y", "x"), ("z", "core")
+    near, far = ("y", "x"), ("core", "z")
     pairs = add_pairs(exchange(pairs, near), 16)
     pairs = add_pairs(exchange(pairs, far), 32)
     pairs = exchange(pairs, near)

time: 86.6 us -> 85.1 us (0.983)
  blocking collectives: 65 us -> 63.6 us
  Pallas kernels: 10.2 us -> 9 us
  starting transfers between devices: 7.27 us -> 8.28 us
    all_to_all x4, blocking collectives: 65 us -> 63.6 us  [exchange(): return lax.all_to_all(x, axes, 0, 0, tiled=True)]
    ppermute x1, starting transfers between devices: 7.27 us -> 8.28 us  [per_device(): got = lax.ppermute(partial[:HALF], 'core', [(0, 1), (1, 0)])]
    pallas_call x1, Pallas kernels: 3.58 us -> 2.57 us  [partial_sketch(): pl.pallas_call(sketch_kernel, out_shape=jax.ShapeDtypeStruct((RB + 1, til...]
where the time goes in v7:
time: 85.1 us; the launch traced here: 84.7 us
  blocking collectives  63.6 us (75%)
  Pallas kernels  9 us (11%)
  starting transfers between devices  8.28 us (10%)
  waiting for transfers between devices  2.26 us (3%)
  between operations  1.32 us (2%)
    all_to_all x4, blocking collectives, exchange(): return lax.all_to_all(x, axes, 0, 0, tiled=True)  63.6 us
    ppermute x1, starting transfers between devices, per_device(): got = lax.ppermute(partial[:HALF], 'core', [(0, 1), (1, 0)])  8.28 us
    pallas_call x1, Pallas kernels, finish(): pl.pallas_call(functools.partial(finish_kernel, scale), out_shape=(jax.Sh...  5.75 us
    pallas_call x1, Pallas kernels, partial_sketch(): pl.pallas_call(sketch_kernel, out_shape=jax.ShapeDtypeStruct((RB + 1, til...  2.57 us
    ppermute x1, waiting for transfers between devices, per_device(): got = lax.ppermute(partial[:HALF], 'core', [(0, 1), (1, 0)])  2.26 us
  transfers between devices with their start and end apart: 1, of which 1 were waited for; matrix products, arithmetic and copies ran while one was open for 0% of the time, Pallas kernels for 0%

profile of v7, /device:TPU:1, one launch (start us, length us, event | category | flops | bytes accessed | tf_op | source)
XLA Modules:
  0.0 84.7 jit_solution(18016184446438291542)
XLA Ops:
  1.3 2.6 %sketch.1 = f32[33,128,128]{2,1,0:T(8,128)S(1)} custom-call(s32[1,1]{1,0:T(1,128)S(6)} %copy.7.count, s32[2,112]{1,0:T(2,128)} %bitcast.15, bf16[112,128,128]{2,1,0:T(8,128)(2,1)} %tiles.1, bf16[4096,128]{1,0:T(8,128)(2,1)} %omega.1), custom_call_target="tpu_custom_call" | custom-call | tf_op jit(solution)/shard_map/sketch/pallas_call | solution.py:92
  3.9 0.1 slice.9
  3.9 8.3 %collective-permute-start = (f32[16,128,128]{2,1,0:T(8,128)S(1)}, f32[16,128,128]{2,1,0:T(8,128)S(1)}, u32[]{:S(2)}, u32[]{:S(2)}) collective-permute-start(f32[16,128,128]{2,1,0:T(8,128)S(1)} %slice.9), channel_id=1, source_target_pairs={{0,1},{1,0},{2,3},{3,2},{4,5},{5,4},{6,7},{7,6},{8,9},{9,8},{10,11... | collective-permute-start | bytes 3145736 | tf_op jit(solution)/shard_map/ppermute | solution.py:343
  12.2 2.3 %collective-permute-done = f32[16,128,128]{2,1,0:T(8,128)S(1)} collective-permute-done((f32[16,128,128]{2,1,0:T(8,128)S(1)}, f32[16,128,128]{2,1,0:T(8,128)S(1)}, u32[]{:S(2)}, u32[]{:S(2)}) %collective-permute-start) | collective-permute-done | bytes 1048608 | tf_op jit(solution)/shard_map/ppermute | solution.py:343
  14.5 0.1 slice_add_fusion
  14.6 17.3 %all_to_all.38 = f32[16,128,128]{2,1,0:T(8,128)S(1)} all-to-all(f32[16,128,128]{2,1,0:T(8,128)S(1)} %slice_add_fusion), channel_id=1, replica_groups=mesh['z'=8,'y'=8,'x'=4,'core'=2] {'x'}, dimensions={0} | all-to-all | bytes 2097152 | tf_op jit(solution)/shard_map/all_to_all | solution.py:336
  31.9 0.6 gram.1
  32.5 13.7 %all_to_all.39 = f32[32,8,128]{2,1,0:T(8,128)S(1)} all-to-all(f32[32,8,128]{2,1,0:T(8,128)S(1)} %bitcast.14), channel_id=1, replica_groups=mesh['z'=8,'y'=8,'x'=4,'core'=2] {'y','x'}, dimensions={0} | all-to-all | bytes 262144 | tf_op jit(solution)/shard_map/all_to_all | solution.py:336
  46.2 0.1 add_pairs.2
  46.3 20.3 %all_to_all.40 = f32[16,8,128]{2,1,0:T(8,128)S(1)} all-to-all(f32[16,8,128]{2,1,0:T(8,128)S(1)} %bitcast.12), channel_id=1, replica_groups=mesh['z'=8,'y'=8,'x'=4,'core'=2] {'core','z'}, dimensions={0} | all-to-all | bytes 131072 | tf_op jit(solution)/shard_map/all_to_all | solution.py:336
  66.6 12.4 %all_to_all.41 = f32[32,8,128]{2,1,0:T(8,128)S(1)} all-to-all(f32[32,8,128]{2,1,0:T(8,128)S(1)} %bitcast.11), channel_id=1, replica_groups=mesh['z'=8,'y'=8,'x'=4,'core'=2] {'y','x'}, dimensions={0} | all-to-all | bytes 262144 | tf_op jit(solution)/shard_map/all_to_all | solution.py:336
  79.0 5.7 %finish.1 = (f32[512,128]{1,0:T(8,128)}, f32[128,128]{1,0:T(8,128)}, f32[128,128]{1,0:T(8,128)}) custom-call(f32[256,128]{1,0:T(8,128)S(1)} %bitcast.9, f32[512,128]{1,0:T(8,128)S(1)} %get-tuple-element.6.sketch), custom_call_target="tpu_custom_call" | custom-call | tf_op jit(solution)/shard_map/finish/pallas_call | solution.py:325
  (1 shorter events, 0.0 us)
Async XLA Ops:
  3.9 10.6 %collective-permute-start = (f32[16,128,128]{2,1,0:T(8,128)S(1)}, f32[16,128,128]{2,1,0:T(8,128)S(1)}, u32[]{:S(2)}, u32[]{:S(2)}) collective-permute-start(f32[16,128,128]{2,1,0:T(8,128)S(1)} %slice.9), channel_id=1, source_target_pairs={{0,1},{1,0},{2,3},{3,2},{4,5},{5,4},{6,7},{7,6},{8,9},{9,8},{10,11... | collective-permute-start | bytes 3145736 | tf_op jit(solution)/shard_map/ppermute | solution.py:343
